TPU v7x, 32 devices: a whole 2x2x4 slice. The times are simulated.
32 devices in a mesh: section: 2 (over x), dp: 8 (over z, y), context: 2 (over core).
Axes of the slice: x: 2, y: 2, z: 4, core: 2. Of those that a mesh axis runs over, the one named last changes fastest.
Arguments:
- hidden_in: bfloat16 [32, 1024, 384], P('dp', 'context'), may hold values from -6 to 6
- cotangent: bfloat16 [32, 1024, 384], P('dp', 'context'), may hold values from -6 to 6
- ada_w: bfloat16 [2, 384, 2304], P('section', 'dp'), may hold values from -0.3125 to 0.3125
- ada_b: bfloat16 [2, 2304], P('section', 'dp'), may hold values from -1.5 to 1.5
- qkv_w: bfloat16 [2, 384, 1152], P('section', 'dp'), may hold values from -0.3125 to 0.3125
- proj_w: bfloat16 [2, 384, 384], P('section', 'dp'), may hold values from -0.625 to 0.625
- mlp_in_w: bfloat16 [2, 384, 1536], P('section', 'dp'), may hold values from -0.3125 to 0.3125
- mlp_out_w: bfloat16 [2, 1536, 384], P('section', 'dp'), may hold values from -0.15625 to 0.15625
- class_table: bfloat16 [1001, 384], P(None, 'dp'), may hold values from -6 to 6
- timesteps: int32 [32], P('dp'), may hold values from 0 to 999
- labels: int32 [32], P('dp'), may hold values from 0 to 1000
Outputs:
- hidden_states: bfloat16 [2, 32, 1024, 384], P('section', 'dp', 'context')
- input_grads: bfloat16 [2, 32, 1024, 384], P('section', 'dp', 'context')
- grad_ada_w: float32 [2, 384, 2304], P('section', 'dp')
- grad_ada_b: float32 [2, 2304], P('section', 'dp')
- grad_qkv_w: float32 [2, 384, 1152], P('section', 'dp')
- grad_proj_w: float32 [2, 384, 384], P('section', 'dp')
- grad_mlp_in_w: float32 [2, 384, 1536], P('section', 'dp')
- grad_mlp_out_w: float32 [2, 1536, 384], P('section', 'dp')
- grad_class_table: float32 [1001, 384], P(None, 'dp')
All inputs are finite; a program needn't handle non-finite values.
Results may differ from a plain program's by a relative error of at most 0.017.
Values may be sent and summed in bfloat16 or wider, within the bound.
A program may use at most 448 MiB of HBM per device.

v0:
```python
import math

import jax
import jax.numpy as jnp
from jax import lax
from jax.sharding import PartitionSpec as P

HDIM = 64
MICRO = 4
LAT_MB = 1


eps_norm = 1e-06


def shifted_2(block, axis, distance):
    devices = range(lax.axis_size(axis))
    route = [(i - distance, i) for i in devices if i - distance in devices]
    return lax.ppermute(block, axis, route)


def sinusoid(step_ids, model_width):
    half_width = model_width // 2
    frequency = jnp.exp(-math.log(10000.0) * jnp.arange(half_width, dtype=jnp.float32) / half_width)
    angles = step_ids.astype(jnp.float32)[:, None] * frequency[None, :]
    return jnp.concatenate([jnp.cos(angles), jnp.sin(angles)], axis=1)


def normalize(values):
    center = values - jnp.mean(values, axis=-1, keepdims=True)
    spread = jnp.mean(center * center, axis=-1, keepdims=True)
    return center * lax.rsqrt(spread + eps_norm)


def gelu_tanh(values):
    return jax.nn.gelu(values, approximate=True)


def layer_forward(stream_low, silu_low, weights):
    ada_w, ada_b, qkv_w, proj_w, mlp_in_w, mlp_out_w = weights
    lat_count, tok_rows, model_width = stream_low.shape
    head_count = model_width // HDIM
    modulation = jnp.dot(silu_low, ada_w, preferred_element_type=jnp.float32) + ada_b.astype(
        jnp.float32
    )
    pieces = [
        modulation[:, None, part_no * model_width : (part_no + 1) * model_width]
        for part_no in range(6)
    ]
    stream = stream_low.astype(jnp.float32)
    normed = normalize(stream)
    first_in = (normed * (1.0 + pieces[1]) + pieces[0]).astype(jnp.bfloat16)
    qkv_all = jnp.dot(first_in, qkv_w, preferred_element_type=jnp.float32).astype(jnp.bfloat16)

    def heads_of(part_no):
        return qkv_all[..., part_no * model_width : (part_no + 1) * model_width].reshape(
            lat_count, tok_rows, head_count, HDIM
        )

    queries = heads_of(0)
    keys_all, values_all = (
        lax.all_gather(heads_of(1), "context", axis=1, tiled=True),
        lax.all_gather(heads_of(2), "context", axis=1, tiled=True),
    )
    score_scale = HDIM ** (-0.5)
    scores = (
        jnp.einsum("bqhe,bkhe->bhqk", queries, keys_all, preferred_element_type=jnp.float32)
        * score_scale
    )
    shifted = jnp.exp(scores - jnp.max(scores, axis=-1, keepdims=True))
    probability = shifted / jnp.sum(shifted, axis=-1, keepdims=True)
    prob_low = probability.astype(jnp.bfloat16)
    mixed_heads = jnp.einsum(
        "bhqk,bkhe->bqhe", prob_low, values_all, preferred_element_type=jnp.float32
    )
    mixed_heads = mixed_heads.astype(jnp.bfloat16).reshape(lat_count, tok_rows, model_width)
    attn_out = jnp.dot(mixed_heads, proj_w, preferred_element_type=jnp.float32)
    middle = stream + pieces[2] * attn_out
    normed_two = normalize(middle)
    second_in = (normed_two * (1.0 + pieces[4]) + pieces[3]).astype(jnp.bfloat16)
    hidden = jnp.dot(second_in, mlp_in_w, preferred_element_type=jnp.float32)
    activated = gelu_tanh(hidden).astype(jnp.bfloat16)
    mlp_out = jnp.dot(activated, mlp_out_w, preferred_element_type=jnp.float32)
    output = middle + pieces[5] * mlp_out
    saved_state = (
        stream,
        normed,
        first_in,
        queries,
        keys_all,
        values_all,
        probability,
        prob_low,
        mixed_heads,
        attn_out,
        middle,
        normed_two,
        second_in,
        hidden,
        activated,
        mlp_out,
        pieces,
    )
    return (output, saved_state)


def layer_backward(grad_out, saved_state, silu_low, weights):
    ada_w, ada_b, qkv_w, proj_w, mlp_in_w, mlp_out_w = weights
    (
        stream,
        normed,
        first_in,
        queries,
        keys_all,
        values_all,
        probability,
        prob_low,
        mixed_heads,
        attn_out,
        middle,
        normed_two,
        second_in,
        hidden,
        activated,
        mlp_out,
        pieces,
    ) = saved_state
    lat_count, tok_rows, model_width = stream.shape
    head_count = model_width // HDIM
    score_scale = HDIM ** (-0.5)
    grad_mlp = (pieces[5] * grad_out).astype(jnp.bfloat16)
    grad_mlp_out = jnp.einsum(
        "bsf,bsd->fd", activated, grad_mlp, preferred_element_type=jnp.float32
    )
    grad_act = jnp.einsum("bsd,fd->bsf", grad_mlp, mlp_out_w, preferred_element_type=jnp.float32)
    gelu_back = jax.vjp(gelu_tanh, hidden)[1]
    grad_hidden = gelu_back(grad_act)[0].astype(jnp.bfloat16)
    grad_mlp_in = jnp.einsum(
        "bsd,bsf->df", second_in, grad_hidden, preferred_element_type=jnp.float32
    )
    grad_second = jnp.einsum(
        "bsf,df->bsd", grad_hidden, mlp_in_w, preferred_element_type=jnp.float32
    )
    norm_back_two = jax.vjp(normalize, middle)[1]
    grad_middle = grad_out + norm_back_two(grad_second * (1.0 + pieces[4]))[0]
    grad_attn = (pieces[2] * grad_middle).astype(jnp.bfloat16)
    grad_proj = jnp.einsum(
        "bsc,bsd->cd", mixed_heads, grad_attn, preferred_element_type=jnp.float32
    )
    grad_mixed = jnp.einsum("bsd,cd->bsc", grad_attn, proj_w, preferred_element_type=jnp.float32)
    grad_mixed = grad_mixed.astype(jnp.bfloat16).reshape(lat_count, tok_rows, head_count, HDIM)
    grad_prob = jnp.einsum(
        "bqhe,bkhe->bhqk", grad_mixed, values_all, preferred_element_type=jnp.float32
    )
    grad_values = jnp.einsum(
        "bhqk,bqhe->bkhe", prob_low, grad_mixed, preferred_element_type=jnp.float32
    )
    grad_scores = probability * (
        grad_prob - jnp.sum(probability * grad_prob, axis=-1, keepdims=True)
    )
    grad_scores = grad_scores.astype(jnp.bfloat16)
    grad_queries = (
        jnp.einsum("bhqk,bkhe->bqhe", grad_scores, keys_all, preferred_element_type=jnp.float32)
        * score_scale
    )
    grad_keys = (
        jnp.einsum("bhqk,bqhe->bkhe", grad_scores, queries, preferred_element_type=jnp.float32)
        * score_scale
    )
    own_keys, own_values = (
        lax.psum_scatter(grad_keys, "context", scatter_dimension=1, tiled=True),
        lax.psum_scatter(grad_values, "context", scatter_dimension=1, tiled=True),
    )
    grad_qkv = jnp.concatenate(
        [
            grad_part.reshape(lat_count, tok_rows, model_width)
            for grad_part in (grad_queries, own_keys, own_values)
        ],
        axis=-1,
    ).astype(jnp.bfloat16)
    grad_wqkv = jnp.einsum("bsd,bse->de", first_in, grad_qkv, preferred_element_type=jnp.float32)
    grad_first = jnp.einsum("bse,de->bsd", grad_qkv, qkv_w, preferred_element_type=jnp.float32)
    norm_back_one = jax.vjp(normalize, stream)[1]
    grad_stream = grad_middle + norm_back_one(grad_first * (1.0 + pieces[1]))[0]
    local_mod = jnp.concatenate(
        [
            jnp.sum(grad_first, axis=1),
            jnp.sum(grad_first * normed, axis=1),
            jnp.sum(grad_middle * attn_out, axis=1),
            jnp.sum(grad_second, axis=1),
            jnp.sum(grad_second * normed_two, axis=1),
            jnp.sum(grad_out * mlp_out, axis=1),
        ],
        axis=-1,
    )
    grad_mod = lax.psum(local_mod, "context")
    grad_ada = jnp.einsum(
        "ld,le->de", silu_low.astype(jnp.float32), grad_mod, precision=lax.Precision.HIGHEST
    )
    grad_bias = jnp.sum(grad_mod, axis=0)
    grad_silu = jnp.einsum(
        "le,de->ld", grad_mod, ada_w.astype(jnp.float32), precision=lax.Precision.HIGHEST
    )
    return (
        grad_stream,
        (grad_ada, grad_bias, grad_wqkv, grad_proj, grad_mlp_in, grad_mlp_out),
        grad_silu,
    )


def pick_block(buffer, block_no):
    return lax.dynamic_index_in_dim(buffer, block_no, 0, keepdims=False)


def put_block(buffer, new_value, block_no, is_valid):
    chosen = jnp.where(is_valid, new_value, pick_block(buffer, block_no))
    return lax.dynamic_update_index_in_dim(buffer, chosen, block_no, 0)


def stack_ticks(*members):
    return jnp.stack(members)


def per_device(
    hidden_in,
    cotangent,
    ada_w,
    ada_b,
    qkv_w,
    proj_w,
    mlp_in_w,
    mlp_out_w,
    class_table,
    timesteps,
    labels,
):
    section_id = lax.axis_index("section")
    lead_mask = (lax.axis_index("context") == 0).astype(jnp.float32)
    gathered = (
        lax.all_gather(ada_w, "dp", axis=1, tiled=True),
        lax.all_gather(ada_b, "dp", axis=1, tiled=True),
        lax.all_gather(qkv_w, "dp", axis=1, tiled=True),
        lax.all_gather(proj_w, "dp", axis=1, tiled=True),
        lax.all_gather(mlp_in_w, "dp", axis=1, tiled=True),
        lax.all_gather(mlp_out_w, "dp", axis=1, tiled=True),
        lax.all_gather(class_table, "dp", axis=1, tiled=True),
    )
    weights = tuple((member[0] for member in gathered[:6]))
    class_rows = gathered[6]
    lat_local, tok_rows, model_width = hidden_in.shape
    one_hot = (labels[:, None] == jnp.arange(class_rows.shape[0], dtype=jnp.int32)[None, :]).astype(
        jnp.bfloat16
    )
    condition = sinusoid(timesteps, model_width) + jnp.dot(
        one_hot, class_rows, preferred_element_type=jnp.float32
    )
    silu_low = jax.nn.silu(condition).astype(jnp.bfloat16)
    block_shape = (MICRO, LAT_MB, tok_rows, model_width)
    stream_blocks = hidden_in.reshape(block_shape)
    cot_blocks = cotangent.reshape(block_shape)
    cond_blocks = condition.reshape(MICRO, LAT_MB, model_width)
    silu_blocks = silu_low.reshape(MICRO, LAT_MB, model_width)
    hot_blocks = one_hot.reshape(MICRO, LAT_MB, class_rows.shape[0])
    inputs_kept = stream_blocks
    outputs_kept = jnp.zeros(block_shape, jnp.bfloat16)
    last_out = jnp.zeros(block_shape[1:], jnp.bfloat16)
    state_list = []
    for tick_no in range(MICRO + 1):
        arrived = last_out
        if tick_no > 0:
            arrived = shifted_2(last_out, "section", 1)
        offset = tick_no - section_id
        block_no = jnp.clip(offset, 0, MICRO - 1)
        is_valid = (offset >= 0) & (offset < MICRO)
        stream_low = jnp.where(section_id == 0, stream_blocks[min(tick_no, MICRO - 1)], arrived)
        output, saved_state = layer_forward(stream_low, pick_block(silu_blocks, block_no), weights)
        state_list.append(saved_state)
        out_low = output.astype(jnp.bfloat16)
        inputs_kept = put_block(inputs_kept, stream_low, block_no, is_valid)
        outputs_kept = put_block(outputs_kept, out_low, block_no, is_valid)
        last_out = out_low
    stacked_states = jax.tree.map(stack_ticks, *state_list)
    refetched = (
        lax.all_gather(ada_w, "dp", axis=1, tiled=True),
        lax.all_gather(ada_b, "dp", axis=1, tiled=True),
        lax.all_gather(qkv_w, "dp", axis=1, tiled=True),
        lax.all_gather(proj_w, "dp", axis=1, tiled=True),
        lax.all_gather(mlp_in_w, "dp", axis=1, tiled=True),
        lax.all_gather(mlp_out_w, "dp", axis=1, tiled=True),
    )
    weights = tuple((member[0] for member in refetched))
    totals = tuple((jnp.zeros(matrix.shape, jnp.float32) for matrix in weights))
    table_total = jnp.zeros(class_rows.shape, jnp.float32)
    grads_kept = jnp.zeros(block_shape, jnp.bfloat16)
    last_grad = jnp.zeros(block_shape[1:], jnp.bfloat16)
    for tick_no in range(MICRO + 1):
        returned = last_grad
        if tick_no > 0:
            returned = shifted_2(last_grad, "section", -1)
        offset = tick_no - 1 + section_id
        block_no = jnp.clip(offset, 0, MICRO - 1)
        is_valid = (offset >= 0) & (offset < MICRO)
        grad_low = jnp.where(section_id == 1, cot_blocks[min(tick_no, MICRO - 1)], returned)
        silu_block = pick_block(silu_blocks, block_no)
        forward_tick = block_no + section_id
        saved_state = jax.tree.map(lambda buffer: pick_block(buffer, forward_tick), stacked_states)
        grad_stream, weight_grads, grad_silu = layer_backward(
            grad_low.astype(jnp.float32), saved_state, silu_block, weights
        )
        scale_all = is_valid.astype(jnp.float32)
        scale_lead = scale_all * lead_mask
        factors = (scale_lead, scale_lead, scale_all, scale_all, scale_all, scale_all)
        totals = tuple(
            (
                running + scaling * addend
                for running, scaling, addend in zip(totals, factors, weight_grads)
            )
        )
        silu_back = jax.vjp(jax.nn.silu, pick_block(cond_blocks, block_no))[1]
        grad_cond = silu_back(grad_silu)[0]
        hot_block = pick_block(hot_blocks, block_no).astype(jnp.float32)
        table_total = table_total + scale_lead * jnp.einsum(
            "lc,ld->cd", hot_block, grad_cond, precision=lax.Precision.HIGHEST
        )
        grad_out_low = grad_stream.astype(jnp.bfloat16)
        grads_kept = put_block(grads_kept, grad_out_low, block_no, is_valid)
        last_grad = grad_out_low
    stacked = tuple((running[None] for running in totals)) + (table_total,)
    summed = lax.psum(stacked, "context")
    shares = lax.psum_scatter(summed, "dp", scatter_dimension=1, tiled=True)
    table_share = lax.psum(shares[6], "section")
    out_shape = (1, lat_local, tok_rows, model_width)
    return (
        outputs_kept.reshape(out_shape),
        grads_kept.reshape(out_shape),
        shares[0],
        shares[1],
        shares[2],
        shares[3],
        shares[4],
        shares[5],
        table_share,
    )


def solution(mesh):
    in_specs = (
        P("dp", "context", None),
        P("dp", "context", None),
        P("section", "dp", None),
        P("section", "dp"),
        P("section", "dp", None),
        P("section", "dp", None),
        P("section", "dp", None),
        P("section", "dp", None),
        P(None, "dp"),
        P("dp"),
        P("dp"),
    )
    out_specs = (
        P("section", "dp", "context", None),
        P("section", "dp", "context", None),
        P("section", "dp", None),
        P("section", "dp"),
        P("section", "dp", None),
        P("section", "dp", None),
        P("section", "dp", None),
        P("section", "dp", None),
        P(None, "dp"),
    )
    return jax.shard_map(
        per_device, mesh=mesh, in_specs=in_specs, out_specs=out_specs, check_vma=False
    )
```

profile of v0, /device:TPU:0, one launch (start us, length us, event | category | flops | bytes accessed | tf_op | source)
XLA Modules:
  0.0 1390.8 jit_solution(16606984755635475807)
XLA Ops:
  10.2 34.7 %all_gather.56 = bf16[1001,384]{0,1:T(8,128)(2,1)S(1)} all-gather(bf16[1001,48]{0,1:T(8,128)(2,1)} %param.19), channel_id=1, replica_groups=mesh['section'=2,'dp'=8,'context'=2] {'dp'}, dimensions={1}, use_global_device_ids=true | all-gather | bytes 864864 | tf_op jit(solution)/shard_map/all_gather | solution.py:246
  47.7 22.3 %all-reduce = bf16[2304]{0:T(1024)(128)(2,1)S(1)} all-reduce(bf16[2304]{0:T(1024)(128)(2,1)S(1)} %dynamic-update-slice), channel_id=1, replica_groups=mesh['section'=2,'dp'=8,'context'=2] {'dp'}, use_global_device_ids=true, to_apply=%add | all-reduce | flops 2304 | bytes 9216
  72.1 35.9 %all_gather.59 = bf16[1,384,1152]{2,1,0:T(8,128)(2,1)} all-gather(bf16[1,48,1152]{2,1,0:T(8,128)(2,1)S(1)} %copy-done.165), channel_id=1, replica_groups=mesh['section'=2,'dp'=8,'context'=2] {'dp'}, dimensions={1}, use_global_device_ids=true | all-gather | bytes 995328 | tf_op jit(solution)/shard_map/all_gather | solution.py:242
  107.9 31.1 %all_gather.62 = bf16[1,384,384]{2,1,0:T(8,128)(2,1)S(1)} all-gather(bf16[1,48,384]{2,1,0:T(8,128)(2,1)S(1)} %copy-done.178), channel_id=1, replica_groups=mesh['section'=2,'dp'=8,'context'=2] {'dp'}, dimensions={1}, use_global_device_ids=true | all-gather | bytes 331776 | tf_op jit(solution)/shard_map/all_gather | solution.py:243
  158.5 6.5 fusion.770
  165.0 8.2 bitcast_dynamic-update-slice_fusion.9
  182.9 10.1 bitcast_dynamic-update-slice_fusion.4
  221.5 6.5 fusion.775
  228.1 8.6 bitcast_dynamic-update-slice_fusion.8
  257.7 10.4 bitcast_dynamic-update-slice_fusion.3
  282.8 9.0 fusion.780
  291.8 8.7 bitcast_dynamic-update-slice_fusion.7
  319.6 10.5 bitcast_dynamic-update-slice_fusion.2
  344.9 9.0 fusion.785
  353.9 8.6 bitcast_dynamic-update-slice_fusion.6
  378.0 10.4 bitcast_dynamic-update-slice_fusion.1
  403.5 9.0 fusion.790
  412.5 11.6 bitcast_dynamic-update-slice_fusion
  464.3 6.8 fusion.13
  471.1 6.2 fusion.14
  484.6 5.7 fusion.200
  507.3 5.9 fusion.215
  552.3 6.8 fusion.11
  559.0 5.8 fusion.12
  571.0 5.7 fusion.203
  581.7 5.9 fusion.216
  605.4 8.5 collective-permute-done.5
  627.4 6.8 fusion.9
  634.2 5.8 fusion.10
  657.2 5.9 fusion.217
  684.0 9.5 collective-permute-done.6
  707.0 6.8 fusion.7
  713.8 5.8 fusion.8
  725.9 5.2 fusion.209
  736.8 5.9 fusion.218
  764.7 8.5 collective-permute-done.7
  787.8 6.9 fusion.5
  794.7 5.8 fusion.6
  812.5 5.9 fusion.212
  875.6 5.2 fusion.357
  918.3 51.8 %reduce-scatter.48.cloned.1.call-done = f32[1,192,384]{2,1,0:T(8,128)} async-done(((f32[1,1536,384]{2,1,0:T(8,128)}), f32[1,192,384]{2,1,0:T(8,128)}) %reduce-scatter.48.cloned.1.call-update) | async-done | bytes 294928 | tf_op jit(solution)/shard_map/reduce_scatter | solution.py:330
  970.1 71.9 %reduce-scatter.46.cloned.1.call-done = f32[1,48,1536]{2,1,0:T(8,128)} async-done(((f32[1,384,1536]{2,1,0:T(8,128)}), f32[1,48,1536]{2,1,0:T(8,128)}) %reduce-scatter.46.cloned.1.call-update) | async-done | bytes 294928 | tf_op jit(solution)/shard_map/reduce_scatter | solution.py:330
  1042.0 67.6 %reduce-scatter.50.cloned.1.call-done = f32[1001,48]{0,1:T(8,128)} async-done(((f32[1001,384]{0,1:T(8,128)}), f32[1001,48]{0,1:T(8,128)}) %reduce-scatter.50.cloned.1.call-update) | async-done | bytes 192208 | tf_op jit(solution)/shard_map/reduce_scatter | solution.py:330
  1109.6 68.2 %reduce-scatter.42.cloned.1.call-done = f32[1,48,1152]{2,1,0:T(8,128)} async-done(((f32[1,384,1152]{2,1,0:T(8,128)}), f32[1,48,1152]{2,1,0:T(8,128)}) %reduce-scatter.42.cloned.1.call-update) | async-done | bytes 221200 | tf_op jit(solution)/shard_map/reduce_scatter | solution.py:330
  1177.9 82.4 %reduce-scatter.40.cloned.1.call-done = f32[1,48,2304]{2,1,0:T(8,128)} async-done(((f32[1,384,2304]{2,1,0:T(8,128)}), f32[1,48,2304]{2,1,0:T(8,128)}) %reduce-scatter.40.cloned.1.call-update) | async-done | bytes 442384 | tf_op jit(solution)/shard_map/reduce_scatter | solution.py:330
  1272.6 10.8 all-reduce.8.cloned.1.call-done
  1286.1 67.0 %reduce-scatter.52.cloned.1.call-done = f32[288,1]{1,0:T(8,128)} async-done(((f32[2304,1]{1,0:T(8,128)}), f32[288,1]{1,0:T(8,128)}) %reduce-scatter.52.cloned.1.call-update) | async-done | bytes 1168
  1357.1 19.7 %all-reduce.6.cloned.1.call-done = f32[1001,48]{0,1:T(8,128)} async-done(((f32[1001,48]{0,1:T(8,128)}), f32[1001,48]{0,1:T(8,128)}) %all-reduce.6.cloned.1.call-update) | async-done | bytes 192208 | tf_op jit(solution)/shard_map/psum | solution.py:331
  (1159 shorter events, 539.4 us)
Async XLA Ops:
  7.2 64.9 %copy-start.165 = (bf16[1,48,1152]{2,1,0:T(8,128)(2,1)S(1)}, bf16[1,48,1152]{2,1,0:T(8,128)(2,1)}, u32[]{:S(2)}) copy-start(bf16[1,48,1152]{2,1,0:T(8,128)(2,1)} %param.15) | copy-start | bytes 331780
  7.2 138.4 %all-gather.4.cloned.1.call-start = ((), (), s32[]{:S(2)}) async-start(), calls=%async_computation.17 | async-start | bytes 1990656 | tf_op jit(solution)/shard_map/all_gather | solution.py:240
  7.9 169.8 %all-gather.6.cloned.1.call-start = ((), (), s32[]{:S(2)}) async-start(), calls=%async_computation.18 | async-start | bytes 1327104 | tf_op jit(solution)/shard_map/all_gather | solution.py:244
  8.7 184.3 %all-gather.8.cloned.1.call-start = ((), (), s32[]{:S(2)}) async-start(), calls=%async_computation.19 | async-start | bytes 1327104 | tf_op jit(solution)/shard_map/all_gather | solution.py:245
  9.4 503.8 %reduce-scatter.20.cloned.1.call-start = ((), (), s32[]{:S(2)}) async-start(), calls=%async_computation.20 | async-start | bytes 2359296 | tf_op jit(solution)/shard_map/reduce_scatter | solution.py:171
  10.2 97.7 %copy-start.178 = (bf16[1,48,384]{2,1,0:T(8,128)(2,1)S(1)}, bf16[1,48,384]{2,1,0:T(8,128)(2,1)}, u32[]{:S(2)}) copy-start(bf16[1,48,384]{2,1,0:T(8,128)(2,1)} %param.16) | copy-start | bytes 110596
  71.7 103.5 %copy-start.53 = (bf16[1,512,384]{1,2,0:T(8,128)(2,1)}, bf16[1,512,384]{1,2,0:T(8,128)(2,1)S(1)}, u32[]{:S(2)}) copy-start(bf16[1,512,384]{1,2,0:T(8,128)(2,1)S(1)} %copy.240) | copy-start | bytes 1179652
  71.9 103.4 %copy-start.189 = (f32[512]{0:T(512)}, f32[512]{0:T(512)S(1)}, u32[]{:S(2)}) copy-start(f32[512]{0:T(512)S(1)} %broadcast_multiply_fusion.19) | copy-start | bytes 6148
  72.0 103.2 %copy-start.218 = (f32[512]{0:T(512)}, f32[512]{0:T(512)S(1)}, u32[]{:S(2)}) copy-start(f32[512]{0:T(512)S(1)} %add_rsqrt_fusion.9) | copy-start | bytes 6148
  200.0 13.1 collective-permute-start
  207.2 97.5 %copy-start.232 = (f32[384]{0:T(512)}, f32[384]{0:T(512)S(1)}, u32[]{:S(2)}) copy-start(f32[384]{0:T(512)S(1)} %get-tuple-element.68) | copy-start | bytes 4612
  207.2 97.5 %copy-start.233 = (f32[384]{0:T(512)}, f32[384]{0:T(512)S(1)}, u32[]{:S(2)}) copy-start(f32[384]{0:T(512)S(1)} %get-tuple-element.69) | copy-start | bytes 4612
  207.9 127.4 %copy-start.294 = (f32[384]{0:T(512)}, f32[384]{0:T(512)S(1)}, u32[]{:S(2)}) copy-start(f32[384]{0:T(512)S(1)} %get-tuple-element.64) | copy-start | bytes 4612
  207.9 127.4 %copy-start.296 = (f32[384]{0:T(512)}, f32[384]{0:T(512)S(1)}, u32[]{:S(2)}) copy-start(f32[384]{0:T(512)S(1)} %get-tuple-element.65) | copy-start | bytes 4612
  207.9 158.9 %copy-start.234 = (f32[384]{0:T(512)}, f32[384]{0:T(512)S(1)}, u32[]{:S(2)}) copy-start(f32[384]{0:T(512)S(1)} %get-tuple-element.62) | copy-start | bytes 4612
  207.9 158.9 %copy-start.235 = (f32[384]{0:T(512)}, f32[384]{0:T(512)S(1)}, u32[]{:S(2)}) copy-start(f32[384]{0:T(512)S(1)} %get-tuple-element.63) | copy-start | bytes 4612
  250.5 21.6 %collective-permute-start.1 = (bf16[1,512,384]{1,2,0:T(8,128)(2,1)}, bf16[1,512,384]{1,2,0:T(8,128)(2,1)}, u32[]{:S(2)}, u32[]{:S(2)}) collective-permute-start(bf16[1,512,384]{1,2,0:T(8,128)(2,1)} %get-tuple-element.176), channel_id=1, source_target_pairs={{0,16},{1,17},{2,18},{3,19},{4,20},{5,21},{6,22},{7,23},{8,24},{9,... | collective-permute-start | bytes 1179656 | tf_op jit(solution)/shard_map/ppermute | solution.py:19
  314.4 19.6 %collective-permute-start.2 = (bf16[1,512,384]{1,2,0:T(8,128)(2,1)}, bf16[1,512,384]{1,2,0:T(8,128)(2,1)}, u32[]{:S(2)}, u32[]{:S(2)}) collective-permute-start(bf16[1,512,384]{1,2,0:T(8,128)(2,1)} %get-tuple-element.174), channel_id=1, source_target_pairs={{0,16},{1,17},{2,18},{3,19},{4,20},{5,21},{6,22},{7,23},{8,24},{9,... | collective-permute-start | bytes 1179656 | tf_op jit(solution)/shard_map/ppermute | solution.py:19
  376.3 14.9 %collective-permute-start.3 = (bf16[1,512,384]{1,2,0:T(8,128)(2,1)S(1)}, bf16[1,512,384]{1,2,0:T(8,128)(2,1)S(1)}, u32[]{:S(2)}, u32[]{:S(2)}) collective-permute-start(bf16[1,512,384]{1,2,0:T(8,128)(2,1)S(1)} %get-tuple-element.172), channel_id=1, source_target_pairs={{0,16},{1,17},{2,18},{3,19},{4,20},{5,21},{6,22},{7,23},{8,24},{9,... | collective-permute-start | bytes 1179656 | tf_op jit(solution)/shard_map/ppermute | solution.py:19
  483.6 31.5 %reduce-scatter.22.cloned.1.call-start = ((), (), s32[]{:S(2)}) async-start(), calls=%async_computation.21 | async-start | bytes 2359296 | tf_op jit(solution)/shard_map/reduce_scatter | solution.py:172
  490.3 97.2 %reduce-scatter.24.cloned.1.call-start = ((), (), s32[]{:S(2)}) async-start(), calls=%async_computation.22 | async-start | bytes 2359296 | tf_op jit(solution)/shard_map/reduce_scatter | solution.py:171
  527.0 13.4 collective-permute-start.4
  570.9 18.6 %reduce-scatter.26.cloned.1.call-start = ((), (), s32[]{:S(2)}) async-start(), calls=%async_computation.23 | async-start | bytes 2359296 | tf_op jit(solution)/shard_map/reduce_scatter | solution.py:172
  576.7 86.4 %reduce-scatter.28.cloned.1.call-start = ((), (), s32[]{:S(2)}) async-start(), calls=%async_computation.24 | async-start | bytes 2359296 | tf_op jit(solution)/shard_map/reduce_scatter | solution.py:171
  601.3 12.6 collective-permute-start.5
  646.0 22.2 %reduce-scatter.30.cloned.1.call-start = ((), (), s32[]{:S(2)}) async-start(), calls=%async_computation.25 | async-start | bytes 2359296 | tf_op jit(solution)/shard_map/reduce_scatter | solution.py:172
  651.3 91.3 %reduce-scatter.32.cloned.1.call-start = ((), (), s32[]{:S(2)}) async-start(), calls=%async_computation.26 | async-start | bytes 2359296 | tf_op jit(solution)/shard_map/reduce_scatter | solution.py:171
  680.0 13.5 collective-permute-start.6
  706.4 50.7 %copy-start.32 = (f32[512,384]{0,1:T(8,128)}, f32[512,384]{0,1:T(8,128)S(1)}, u32[]{:S(2)}) copy-start(f32[512,384]{0,1:T(8,128)S(1)} %get-tuple-element.130) | copy-start | bytes 2359300
  725.7 22.2 %reduce-scatter.34.cloned.1.call-start = ((), (), s32[]{:S(2)}) async-start(), calls=%async_computation.27 | async-start | bytes 2359296 | tf_op jit(solution)/shard_map/reduce_scatter | solution.py:172
  731.1 153.8 %reduce-scatter.36.cloned.1.call-start = ((), (), s32[]{:S(2)}) async-start(), calls=%async_computation.28 | async-start | bytes 2359296 | tf_op jit(solution)/shard_map/reduce_scatter | solution.py:171
  759.6 13.6 collective-permute-start.7
  806.9 79.3 %reduce-scatter.38.cloned.1.call-start = ((), (), s32[]{:S(2)}) async-start(), calls=%async_computation.29 | async-start | bytes 2359296 | tf_op jit(solution)/shard_map/reduce_scatter | solution.py:172
  818.4 99.9 %reduce-scatter.44.cloned.1.call-start = ((), (), s32[]{:S(2)}) async-start(), calls=%async_computation.33 | async-start | bytes 663552 | tf_op jit(solution)/shard_map/reduce_scatter | solution.py:330
  835.6 134.5 %reduce-scatter.48.cloned.1.call-start = ((), (), s32[]{:S(2)}) async-start(), calls=%async_computation.35 | async-start | bytes 2654208 | tf_op jit(solution)/shard_map/reduce_scatter | solution.py:330
  847.7 194.2 %reduce-scatter.46.cloned.1.call-start = ((), (), s32[]{:S(2)}) async-start(), calls=%async_computation.34 | async-start | bytes 2654208 | tf_op jit(solution)/shard_map/reduce_scatter | solution.py:330
  875.3 234.3 %reduce-scatter.50.cloned.1.call-start = ((), (), s32[]{:S(2)}) async-start(), calls=%async_computation.36 | async-start | bytes 1769472 | tf_op jit(solution)/shard_map/reduce_scatter | solution.py:330
  904.8 273.1 %reduce-scatter.42.cloned.1.call-start = ((), (), s32[]{:S(2)}) async-start(), calls=%async_computation.32 | async-start | bytes 1990656 | tf_op jit(solution)/shard_map/reduce_scatter | solution.py:330
  914.7 345.6 %reduce-scatter.40.cloned.1.call-start = ((), (), s32[]{:S(2)}) async-start(), calls=%async_computation.31 | async-start | bytes 3981312 | tf_op jit(solution)/shard_map/reduce_scatter | solution.py:330
  918.2 342.2 %copy-start.126 = (bf16[1,1,512,384]{2,3,1,0:T(8,128)(2,1)S(1)}, bf16[1,1,512,384]{2,3,1,0:T(8,128)(2,1)}, u32[]{:S(2)}) copy-start(bf16[1,1,512,384]{2,3,1,0:T(8,128)(2,1)} %get-tuple-element.171) | copy-start | bytes 1179652
  918.2 342.4 %copy-start.66 = (bf16[4,1,512,384]{3,2,0,1:T(8,128)(2,1)S(1)}, bf16[4,1,512,384]{3,2,0,1:T(8,128)(2,1)}, u32[]{:S(2)}) copy-start(bf16[4,1,512,384]{3,2,0,1:T(8,128)(2,1)} %constant_dynamic-update-slice_fusion.67) | copy-start | bytes 4718596
  918.2 345.8 %copy-start.306 = (f32[384]{0:T(512)S(1)}, f32[384]{0:T(512)}, u32[]{:S(2)}) copy-start(f32[384]{0:T(512)} %get-tuple-element.55) | copy-start | bytes 4612
  918.2 365.2 %all-reduce.8.cloned.1.call-start = ((), (), s32[]{:S(2)}) async-start(), calls=%async_computation.38 | async-start | bytes 3047424 | tf_op jit(solution)/shard_map/psum | solution.py:329
  1260.3 92.8 %reduce-scatter.52.cloned.1.call-start = ((), (), s32[]{:S(2)}) async-start(), calls=%async_computation.37 | async-start | bytes 1327104
  1269.7 107.0 %all-reduce.6.cloned.1.call-start = ((), (), s32[]{:S(2)}) async-start(), calls=%async_computation.30 | async-start | bytes 393216 | tf_op jit(solution)/shard_map/psum | solution.py:331
  1283.4 93.4 %copy-start.140 = (f32[1,48,2304]{2,1,0:T(8,128)S(1)}, f32[1,48,2304]{2,1,0:T(8,128)}, u32[]{:S(2)}) copy-start(f32[1,48,2304]{2,1,0:T(8,128)} %get-tuple-element.343) | copy-start | bytes 1327108
  1283.4 98.0 %copy-start.161 = (f32[1,192,384]{2,1,0:T(8,128)S(1)}, f32[1,192,384]{2,1,0:T(8,128)}, u32[]{:S(2)}) copy-start(f32[1,192,384]{2,1,0:T(8,128)} %get-tuple-element.348) | copy-start | bytes 884740
  1285.0 95.7 %copy-start.162 = (f32[1,48,1536]{2,1,0:T(8,128)S(1)}, f32[1,48,1536]{2,1,0:T(8,128)}, u32[]{:S(2)}) copy-start(f32[1,48,1536]{2,1,0:T(8,128)} %get-tuple-element.347) | copy-start | bytes 884740
  (308 other events, 2427.3 us)
Sparse Core Ops, SparseCore 0:
  10.2 51.5 all-gather.3
  64.0 44.3 all-gather.5
  110.6 39.9 all-gather.7
  483.7 5.2 reduce-scatter.19
  491.8 10.2 reduce-scatter.21
  571.0 4.9 reduce-scatter.23
  578.3 10.2 reduce-scatter.25
  646.2 9.3 reduce-scatter.27
  657.9 10.2 reduce-scatter.29
  725.8 9.3 reduce-scatter.31
  737.5 10.2 reduce-scatter.33
  807.0 9.4 reduce-scatter.35
  818.8 10.2 reduce-scatter.37
  835.8 62.4 reduce-scatter.43
  902.0 68.0 reduce-scatter.47
  973.9 68.0 reduce-scatter.45
  1045.6 63.9 reduce-scatter.49
  1112.9 64.8 reduce-scatter.41
  1181.9 78.3 reduce-scatter.39
  1263.1 20.2 all-reduce.7
  1287.2 65.8 reduce-scatter.51
  1355.5 21.2 all-reduce.5
where the time goes:
time: 1400 us; the launch traced here: 1390 us
  waiting for transfers between devices  479 us (34%)
  matrix products  304 us (22%)
  other arithmetic  252 us (18%)
  local copies, waits for them, and re-layouts  160 us (11%)
  blocking collectives  157 us (11%)
  between operations  20 us (1%)
  starting transfers between devices  19 us (1%)
    reduce_scatter x6, waiting for transfers between devices, per_device(): shares = lax.psum_scatter(summed, 'dp', scatter_dimension=1, tiled=True)  342 us
    unnamed x28, other arithmetic  96.6 us
    unnamed x23, waiting for transfers between devices  69.4 us
    unnamed x716, local copies, waits for them, and re-layouts  55.8 us
    dynamic_slice x36, local copies, waits for them, and re-layouts, pick_block(): return lax.dynamic_index_in_dim(buffer, block_no, 0, keepdims=False)  50.7 us
    sub x5, matrix products, layer_forward(): shifted = jnp.exp(scores - jnp.max(scores, axis=-1, keepdims=True))  39.9 us
    all_gather x1, blocking collectives, per_device(): lax.all_gather(qkv_w, 'dp', axis=1, tiled=True)  35.9 us
    all_gather x1, blocking collectives, per_device(): lax.all_gather(class_table, 'dp', axis=1, tiled=True)  34.7 us
  transfers between devices with their start and end apart: 30, of which 14 were waited for; matrix products, arithmetic and copies ran while one was open for 24% of the time, Pallas kernels for 0%

commit v1 on v0

v1 whole, which is shorter than its diff:
```python
import functools
import math

import jax
import jax.numpy as jnp
from jax import lax
from jax.experimental import pallas as pl
from jax.experimental.pallas import tpu as pltpu
from jax.sharding import PartitionSpec as P

HDIM = 64
PAIR = 2 * HDIM
TILE = 256
EPS = 1e-06
SCALE = HDIM ** (-0.5)
GC = math.sqrt(2.0 / math.pi)
GA = 0.044715
F32 = jnp.float32
BF16 = jnp.bfloat16
NT = (((1,), (1,)), ((), ()))
TN = (((0,), (0,)), ((), ()))
HIGH = lax.Precision.HIGHEST


def mm(a, b, dims=(((1,), (0,)), ((), ()))):
    return lax.dot_general(a, b, dims, preferred_element_type=F32)


def norm_of(v):
    center = v - jnp.mean(v, axis=-1, keepdims=True)
    rs = lax.rsqrt(jnp.mean(center * center, axis=-1, keepdims=True) + EPS)
    return center * rs, rs


def norm_back(n, rs, u):
    return rs * (
        u - jnp.mean(u, axis=-1, keepdims=True) - n * jnp.mean(u * n, axis=-1, keepdims=True)
    )


def row_loop(count, body):
    def step(i, carry):
        body(pl.ds(pl.multiple_of(i * TILE, TILE), TILE))
        return carry

    lax.fori_loop(0, count // TILE, step, 0)


def head_masks(rows):
    lane = lax.broadcasted_iota(jnp.int32, (rows, PAIR), 1)
    return [lane < HDIM, lane >= HDIM]


def fwd_kernel(x_ref, mod_ref, wqkv, wproj, wmi, wmo, y_ref, qkv_ref, lse_ref, mix_ref, mid_ref, ao_ref, mo_ref, vt_ref):
    tok, d = x_ref.shape
    mod = mod_ref[...]
    sh1, sc1, g1, sh2, sc2, g2 = [mod[i : i + 1] for i in range(6)]

    def project(rows):
        n, _ = norm_of(x_ref[rows, :].astype(F32))
        first = (n * (1.0 + sc1) + sh1).astype(BF16)
        qkv = mm(first, wqkv[...])
        qkv_ref[rows, :] = qkv.astype(BF16)
        vt_ref[:, rows] = qkv[:, 2 * d :].T.astype(BF16)

    row_loop(tok, project)
    lse_ref[...] = jnp.zeros_like(lse_ref)
    masks = head_masks(TILE)
    for p in range(d // PAIR):
        lo = p * PAIR

        def attend(rows, p=p, lo=lo):
            q = qkv_ref[rows, lo : lo + PAIR] * SCALE
            k = qkv_ref[:, d + lo : d + lo + PAIR]
            outs = []
            for h in range(2):
                qm = jnp.where(masks[h], q, jnp.zeros_like(q))
                st = mm(k, qm, NT)
                top = jnp.max(st, axis=0, keepdims=True)
                e = jnp.exp(st - top)
                total = jnp.sum(e, axis=0, keepdims=True)
                row = 2 * p + h
                lse_ref[row : row + 1, rows] = top + jnp.log(total)
                ot = mm(vt_ref[lo + h * HDIM : lo + (h + 1) * HDIM, :], e.astype(BF16))
                outs.append(ot / total)
            mix_ref[rows, lo : lo + PAIR] = jnp.concatenate(outs, axis=0).T.astype(BF16)

        row_loop(tok, attend)

    def feed(rows):
        ao = mm(mix_ref[rows, :], wproj[...])
        mid = x_ref[rows, :].astype(F32) + g1 * ao
        ao_ref[rows, :] = ao.astype(BF16)
        mid_ref[rows, :] = mid
        n, _ = norm_of(mid)
        second = (n * (1.0 + sc2) + sh2).astype(BF16)
        hid = mm(second, wmi[...])
        act = 0.5 * hid * (1.0 + jnp.tanh(GC * (hid + GA * hid * hid * hid)))
        mo = mm(act.astype(BF16), wmo[...])
        mo_ref[rows, :] = mo.astype(BF16)
        y_ref[rows, :] = (mid + g2 * mo).astype(BF16)

    row_loop(tok, feed)


def bwd_kernel(g_ref, x_ref, mod_ref, wqkv, wproj, wmi, wmo, qkv_ref, lse_ref, mix_ref, mid_ref, ao_ref, mo_ref,
               gin_ref, gmod_ref, dqkvw_ref, dproj_ref, dmi_ref, dmo_ref,
               aqkv, aproj, ami, amo, kt_ref, gmid_ref, gmx_ref, delta_ref, dqkv_ref, dk_acc, dv_acc):
    tok, d = x_ref.shape
    heads = d // HDIM
    mod = mod_ref[...]
    sh1, sc1, g1, sh2, sc2, g2 = [mod[i : i + 1] for i in range(6)]
    for acc in (gmod_ref, aqkv, aproj, ami, amo):
        acc[...] = jnp.zeros_like(acc)
    sel = (
        lax.broadcasted_iota(jnp.int32, (8, d), 1) // HDIM == lax.broadcasted_iota(jnp.int32, (8, d), 0)
    ).astype(F32)

    def add_mod(i, value):
        gmod_ref[i : i + 1, :] += jnp.sum(value, axis=0, keepdims=True)

    def feed_back(rows):
        kt_ref[:, rows] = qkv_ref[rows, d : 2 * d].astype(F32).T.astype(BF16)
        n, rs = norm_of(mid_ref[rows, :])
        second = (n * (1.0 + sc2) + sh2).astype(BF16)
        hid = mm(second, wmi[...])
        sq = hid * hid
        th = jnp.tanh(GC * (hid + GA * hid * sq))
        half = 0.5 * (1.0 + th)
        act = (hid * half).astype(BF16)
        slope = half + 0.5 * hid * (1.0 - th * th) * (GC * (1.0 + 3.0 * GA * sq))
        g = g_ref[rows, :].astype(F32)
        gm = (g2 * g).astype(BF16)
        amo[...] += mm(act, gm, TN)
        gh = (mm(gm, wmo[...], NT) * slope).astype(BF16)
        ami[...] += mm(second, gh, TN)
        gs = mm(gh, wmi[...], NT)
        add_mod(3, gs)
        add_mod(4, gs * n)
        add_mod(5, g * mo_ref[rows, :].astype(F32))
        gmid = g + norm_back(n, rs, gs * (1.0 + sc2))
        gmid_ref[rows, :] = gmid
        add_mod(2, gmid * ao_ref[rows, :].astype(F32))
        ga = (g1 * gmid).astype(BF16)
        mix = mix_ref[rows, :]
        aproj[...] += mm(mix, ga, TN)
        gmx = mm(ga, wproj[...], NT).astype(BF16)
        gmx_ref[rows, :] = gmx
        delta_ref[:, rows] = lax.dot_general(
            sel, gmx.astype(F32) * mix.astype(F32), NT, precision=HIGH, preferred_element_type=F32
        )

    row_loop(tok, feed_back)
    masks = head_masks(TILE)
    for p in range(d // PAIR):
        lo = p * PAIR
        dk_acc[...] = jnp.zeros_like(dk_acc)
        dv_acc[...] = jnp.zeros_like(dv_acc)

        def attend_back(rows, p=p, lo=lo):
            q = qkv_ref[rows, lo : lo + PAIR] * SCALE
            do = gmx_ref[rows, lo : lo + PAIR]
            k = qkv_ref[:, d + lo : d + lo + PAIR]
            v = qkv_ref[:, 2 * d + lo : 2 * d + lo + PAIR]
            outs = []
            for h in range(2):
                row = 2 * p + h
                qm = jnp.where(masks[h], q, jnp.zeros_like(q))
                dom = jnp.where(masks[h], do, jnp.zeros_like(do))
                pt = jnp.exp(mm(k, qm, NT) - lse_ref[row : row + 1, rows])
                dv_acc[...] += mm(pt.astype(BF16), dom)
                ds = (pt * (mm(v, dom, NT) - delta_ref[row : row + 1, rows])).astype(BF16)
                dk_acc[...] += mm(ds, qm)
                outs.append(mm(kt_ref[lo + h * HDIM : lo + (h + 1) * HDIM, :], ds))
            dqkv_ref[rows, lo : lo + PAIR] = (jnp.concatenate(outs, axis=0) * SCALE).T.astype(BF16)

        row_loop(tok, attend_back)
        dqkv_ref[:, d + lo : d + lo + PAIR] = dk_acc[...].astype(BF16)
        dqkv_ref[:, 2 * d + lo : 2 * d + lo + PAIR] = dv_acc[...].astype(BF16)

    def project_back(rows):
        n, rs = norm_of(x_ref[rows, :].astype(F32))
        first = (n * (1.0 + sc1) + sh1).astype(BF16)
        dqkv = dqkv_ref[rows, :]
        aqkv[...] += mm(first, dqkv, TN)
        gf = mm(dqkv, wqkv[...], NT)
        add_mod(0, gf)
        add_mod(1, gf * n)
        gin_ref[rows, :] = (gmid_ref[rows, :] + norm_back(n, rs, gf * (1.0 + sc1))).astype(BF16)

    row_loop(tok, project_back)
    dqkvw_ref[...] = aqkv[...].astype(BF16)
    dproj_ref[...] = aproj[...].astype(BF16)
    dmi_ref[...] = ami[...].astype(BF16)
    dmo_ref[...] = amo[...].astype(BF16)


def vmem(count):
    return [pl.BlockSpec(memory_space=pltpu.VMEM)] * count


def run_forward(x, mod, weights):
    tok, d = x.shape
    sds = jax.ShapeDtypeStruct
    ff = weights[2].shape[1]
    return pl.pallas_call(
        fwd_kernel,
        out_shape=[
            sds((tok, d), BF16),
            sds((tok, 3 * d), BF16),
            sds((8, tok), F32),
            sds((tok, d), BF16),
            sds((tok, d), F32),
            sds((tok, d), BF16),
            sds((tok, d), BF16),
        ],
        in_specs=vmem(6),
        out_specs=vmem(7),
        scratch_shapes=[pltpu.VMEM((d, tok), BF16)],
        compiler_params=pltpu.CompilerParams(vmem_limit_bytes=48 * 2**20),
        cost_estimate=pl.CostEstimate(
            flops=2 * tok * d * (4 * d + 2 * ff + 8 * tok), bytes_accessed=16 * 2**20, transcendentals=0
        ),
    )(x, mod, *weights)


def run_backward(g, x, mod, weights, saved):
    tok, d = x.shape
    sds = jax.ShapeDtypeStruct
    ff = weights[2].shape[1]
    shapes = [(d, 3 * d), (d, d), (d, ff), (ff, d)]
    return pl.pallas_call(
        bwd_kernel,
        out_shape=[sds((tok, d), BF16), sds((8, d), F32)] + [sds(s, BF16) for s in shapes],
        in_specs=vmem(13),
        out_specs=vmem(6),
        scratch_shapes=[pltpu.VMEM(s, F32) for s in shapes]
        + [
            pltpu.VMEM((d, tok), BF16),
            pltpu.VMEM((tok, d), F32),
            pltpu.VMEM((tok, d), BF16),
            pltpu.VMEM((8, tok), F32),
            pltpu.VMEM((tok, 3 * d), BF16),
            pltpu.VMEM((tok, PAIR), F32),
            pltpu.VMEM((tok, PAIR), F32),
        ],
        compiler_params=pltpu.CompilerParams(vmem_limit_bytes=56 * 2**20),
        cost_estimate=pl.CostEstimate(
            flops=4 * tok * d * (4 * d + 3 * ff + 10 * tok), bytes_accessed=24 * 2**20, transcendentals=0
        ),
    )(g, x, mod, *weights, *saved)


def sinusoid(step_ids, model_width):
    half_width = model_width // 2
    frequency = jnp.exp(-math.log(10000.0) * jnp.arange(half_width, dtype=F32) / half_width)
    angles = step_ids.astype(F32)[:, None] * frequency[None, :]
    return jnp.concatenate([jnp.cos(angles), jnp.sin(angles)], axis=1)


def swap_axis(value, axis):
    return lax.ppermute(value, axis, [(0, 1), (1, 0)])


def take_latent(block, section, context):
    pair = lax.dynamic_slice_in_dim(block, 2 * section, 2, 0)
    own = lax.dynamic_index_in_dim(pair, context, 0, keepdims=False)
    other = swap_axis(lax.dynamic_index_in_dim(pair, 1 - context, 0, keepdims=False), "context")
    first = context == 0
    return jnp.concatenate([jnp.where(first, own, other), jnp.where(first, other, own)], axis=0)


def spread_out(zero, one):
    tok, d = zero.shape
    both = jnp.concatenate([zero, one], axis=0).reshape(4, tok // 2, d)
    return lax.all_to_all(both, ("section", "context"), 0, 0, tiled=True)[None]


def per_device(hidden_in, cotangent, ada_w, ada_b, qkv_w, proj_w, mlp_in_w, mlp_out_w, class_table, timesteps, labels):
    section = lax.axis_index("section")
    dp = lax.axis_index("dp")
    context = lax.axis_index("context")
    d = hidden_in.shape[-1]
    cols = class_table.shape[1]

    steps_all = lax.all_gather(timesteps, "dp", tiled=True)
    labels_all = lax.all_gather(labels, "dp", tiled=True)

    def gather(w):
        w = w[0]
        half = w.shape[0] // 2
        mine = lax.dynamic_slice_in_dim(w, context * half, half, 0)
        full = lax.all_gather(mine, ("section", "dp", "context"), axis=0, tiled=True)
        rows = full.shape[0] // 2
        return full[:rows], full[rows:]

    pairs = [gather(w) for w in (qkv_w, proj_w, mlp_in_w, mlp_out_w)]
    weights = [tuple(pair[layer] for pair in pairs) for layer in range(2)]
    hidden = take_latent(hidden_in, section, context)
    cot = take_latent(cotangent, section, context)

    one_hot = (labels_all[:, None] == jnp.arange(class_table.shape[0], dtype=jnp.int32)[None, :]).astype(F32)
    phase = lax.dynamic_slice_in_dim(sinusoid(steps_all, d), dp * cols, cols, 1)
    condition = phase + jnp.dot(one_hot.astype(BF16), class_table, preferred_element_type=F32)
    silu_low = jax.nn.silu(condition).astype(BF16)
    partial = jnp.dot(silu_low, ada_w[0], preferred_element_type=F32)
    wide = ada_b.shape[1]
    bias = lax.dynamic_update_slice_in_dim(
        jnp.zeros((1, partial.shape[1]), F32), ada_b.astype(F32), dp * wide, 1
    )
    mods = lax.psum_scatter(partial + bias, "dp", scatter_dimension=0, tiled=True)
    mods = lax.all_gather(mods, "section")
    mods = lax.dynamic_index_in_dim(mods, 2 * section + context, 1, keepdims=False)
    mods = jnp.pad(mods.reshape(2, 6, d), ((0, 0), (0, 2), (0, 0)))

    passed, *saved0 = run_forward(hidden, mods[0], weights[0])
    second, *saved1 = run_forward(passed, mods[1], weights[1])
    states = spread_out(passed, second)

    def reduce(grads):
        return [lax.psum_scatter(g, ("dp", "context"), scatter_dimension=0, tiled=True) for g in grads]

    g0, gmod1, *wg1 = run_backward(cot, passed, mods[1], weights[1], saved1)
    parts1 = reduce(wg1)
    gin, gmod0, *wg0 = run_backward(g0, hidden, mods[0], weights[0], saved0)
    parts0 = reduce(wg0)
    grads = spread_out(gin, g0)

    upper = section == 1
    shares = []
    for p0, p1 in zip(parts0, parts1):
        other = swap_axis(jnp.where(upper, p0, p1), "section")
        mine = jnp.where(upper, p1, p0).astype(F32) + other.astype(F32)
        shares.append(lax.all_gather(mine, "context", axis=0, tiled=True)[None])

    def all_latents(gmod):
        return lax.all_gather(gmod[:6].reshape(-1), ("dp", "section", "context"))

    gm = jnp.where(upper, all_latents(gmod1), all_latents(gmod0))
    grad_ada = jnp.einsum("ld,le->de", silu_low.astype(F32), gm, precision=HIGH)[None]
    grad_bias = lax.dynamic_slice_in_dim(jnp.sum(gm, axis=0, keepdims=True), dp * wide, wide, 1)
    grad_silu = jnp.einsum("le,de->ld", gm, ada_w[0].astype(F32), precision=HIGH)
    grad_silu = lax.psum(grad_silu, "section")
    grad_cond = jax.vjp(jax.nn.silu, condition)[1](grad_silu)[0]
    table = jnp.einsum("lc,ld->cd", one_hot, grad_cond, precision=HIGH)
    return (states, grads, grad_ada, grad_bias, *shares, table)


def solution(mesh):
    wide = P("section", "dp", None)
    tokens = P("dp", "context", None)
    in_specs = (tokens, tokens, wide, P("section", "dp"), wide, wide, wide, wide, P(None, "dp"), P("dp"), P("dp"))
    stacked = P("section", "dp", "context", None)
    out_specs = (stacked, stacked, wide, P("section", "dp"), wide, wide, wide, wide, P(None, "dp"))
    return jax.shard_map(per_device, mesh=mesh, in_specs=in_specs, out_specs=out_specs, check_vma=False)
```

time: 1400 us -> 824 us (0.59)
  matrix products: 304 us -> 5.41 us
  other arithmetic: 252 us -> 14.1 us
  Pallas kernels: 0 us -> 161 us
  local copies, waits for them, and re-layouts: 160 us -> 29.2 us
  waiting for transfers between devices: 479 us -> 413 us
    dot_general x96 -> x5, matrix products: 264 us -> 5.41 us  [the longest x1 2.13 us: per_device(): jnp.einsum('ld,le->de', silu_low.astype(F32), gm, precision=HIGH)[None]]
    pallas_call x0 -> x4, Pallas kernels: none -> 161 us  [the longest x2 99.5 us: run_backward(): pl.pallas_call(bwd_kernel, out_shape=[sds((tok, d), BF16), sds((8, d), F3...]
    reduce_scatter x16 -> x4, waiting for transfers between devices: 348 us -> 234 us  [reduce(): lax.psum_scatter(g, ('dp', 'context'), scatter_dimension=0, tiled=True)]
    unnamed x28 -> x0, other arithmetic: 96.6 us -> none
    all_gather x3, waiting for transfers between devices: 0.02 us -> 94.8 us  [gather(): lax.all_gather(mine, ('section', 'dp', 'context'), axis=0, tiled=True)]
    reduce_sum x49 -> x1, other arithmetic: 54.7 us -> 0.39 us  [per_device(): jnp.sum(gm, axis=0, keepdims=True)]
    dynamic_slice x36 -> x6, local copies, waits for them, and re-layouts: 50.7 us -> 4.27 us  [the longest x4 3.63 us: gather(): mine = lax.dynamic_slice_in_dim(w, context * half, half, 0)]
    unnamed x716 -> x64, local copies, waits for them, and re-layouts: 55.8 us -> 14.1 us
  transfers between devices with their start and end apart: 30 -> 20, of which waited for: 14 -> 9; matrix products, arithmetic and copies ran while one was open for 24% -> 3% of each run, Pallas kernels for 0% -> 6%
where the time goes in v1:
time: 824 us; the launch traced here: 820 us
  waiting for transfers between devices  413 us (50%)
  blocking collectives  164 us (20%)
  Pallas kernels  161 us (20%)
  local copies, waits for them, and re-layouts  29.2 us (4%)
  between operations  17.7 us (2%)
  starting transfers between devices  15 us (2%)
  other arithmetic  14.1 us (2%)
    reduce_scatter x4, waiting for transfers between devices, reduce(): lax.psum_scatter(g, ('dp', 'context'), scatter_dimension=0, tiled=True)  234 us
    pallas_call x2, Pallas kernels, run_backward(): pl.pallas_call(bwd_kernel, out_shape=[sds((tok, d), BF16), sds((8, d), F3...  99.5 us
    all_gather x3, waiting for transfers between devices, gather(): lax.all_gather(mine, ('section', 'dp', 'context'), axis=0, tiled=True)  94.8 us
    all_gather x2, blocking collectives, all_latents(): return lax.all_gather(gmod[:6].reshape(-1), ('dp', 'section', 'context'))  89.8 us
    unnamed x17, waiting for transfers between devices  83.8 us
    pallas_call x2, Pallas kernels, run_forward(): pl.pallas_call(fwd_kernel, out_shape=[sds((tok, d), BF16), sds((tok, 3 *...  61.5 us
    all_gather x1, blocking collectives, gather(): lax.all_gather(mine, ('section', 'dp', 'context'), axis=0, tiled=True)  40.4 us
  transfers between devices with their start and end apart: 20, of which 9 were waited for; matrix products, arithmetic and copies ran while one was open for 3% of the time, Pallas kernels for 6%

profile of v1, /device:TPU:0, one launch (start us, length us, event | category | flops | bytes accessed | tf_op | source)
XLA Modules:
  0.0 819.7 jit_solution(6937877380595723313)
XLA Ops:
  8.1 1.3 fusion.21
  11.8 13.1 %all-reduce.8 = (s32[32]{0:T(128)S(1)}, s32[32]{0:T(128)S(1)}) all-reduce(s32[32]{0:T(128)S(1)} %dynamic-update-slice.1, s32[32]{0:T(128)S(1)} %dynamic-update-slice), channel_id=1, replica_groups=mesh['section'=2,'dp'=8,'context'=2] {'dp'}, use_global_device_ids=true, to_apply=%add.2 | all-reduce | flops 64 | bytes 512
  26.1 1.1 convolution_add_fusion.1
  28.2 1.4 constant_dynamic-slice_fusion.3
  29.7 1.5 constant_dynamic-slice_fusion.1
  32.0 1.0 dynamic-slice_bitcast_fusion
  33.2 1.0 dynamic-slice_bitcast_fusion.1
  35.5 40.4 %all-gather.2 = bf16[1,768,384]{2,1,0:T(8,128)(2,1)S(1)} all-gather(bf16[1,24,384]{2,1,0:T(8,128)(2,1)S(1)} %constant_dynamic-slice_fusion.2), channel_id=4, replica_groups=mesh['section'=2,'dp'=8,'context'=2] {'section','dp','context'}, dimensions={1}, use_global_device_ids=true | all-gather | bytes 608256 | tf_op jit(solution)/shard_map/all_gather | solution.py:293
  75.9 22.4 %all-reduce.11.cloned.1.call-done = f32[32,2304]{1,0:T(8,128)} async-done(((f32[32,2304]{1,0:T(8,128)}), f32[32,2304]{1,0:T(8,128)}) %all-reduce.11.cloned.1.call-update) | async-done | bytes 294928
  99.2 4.6 all-gather.5
  104.0 1.3 bitcast_select_fusion.1
  105.3 1.0 pad_maximum_fusion.3.g_ref
  106.4 1.8 slice_bitcast_fusion.4
  108.2 38.2 %all-gather.14.cloned.1.call-done = bf16[1,768,1536]{2,1,0:T(8,128)(2,1)} async-done(((bf16[1,24,1536]{2,1,0:T(8,128)(2,1)}), bf16[1,768,1536]{2,1,0:T(8,128)(2,1)}) %all-gather.14.cloned.1.call-update) | async-done | bytes 2359312 | tf_op jit(solution)/shard_map/all_gather | solution.py:293
  146.4 3.2 slice_bitcast_fusion.1
  149.6 56.6 %all-gather.16.cloned.1.call-done = bf16[1,3072,384]{2,1,0:T(8,128)(2,1)} async-done(((bf16[1,96,384]{2,1,0:T(8,128)(2,1)}), bf16[1,3072,384]{2,1,0:T(8,128)(2,1)}) %all-gather.16.cloned.1.call-update) | async-done | bytes 2359312 | tf_op jit(solution)/shard_map/all_gather | solution.py:293
  206.3 3.3 slice_bitcast_fusion
  209.5 30.5 %shard_map.178 = (bf16[1024,384]{1,0:T(8,128)(2,1)S(1)}, bf16[1024,1152]{1,0:T(8,128)(2,1)}, f32[8,1024]{1,0:T(8,128)S(1)}, bf16[1024,384]{1,0:T(8,128)(2,1)S(1)...) custom-call(bf16[1024,384]{1,0:T(8,128)(2,1)S(1)} %pad_maximum_fusion.2.x_ref, ...), custom_call_target="tpu_custom_call" | custom-call | flops 10066329600 | bytes 16777216 | tf_op jit(solution)/shard_map/pallas_call | solution.py:206
  241.9 31.0 %shard_map.179 = (bf16[1024,384]{1,0:T(8,128)(2,1)S(1)}, bf16[1024,1152]{1,0:T(8,128)(2,1)}, f32[8,1024]{1,0:T(8,128)S(1)}, bf16[1024,384]{1,0:T(8,128)(2,1)S(1)...) custom-call(bf16[1024,384]{1,0:T(8,128)(2,1)S(1)} %get-tuple-element.35.x_ref, ...), custom_call_target="tpu_custom_call" | custom-call | flops 10066329600 | bytes 16777216 | tf_op jit(solution)/shard_map/pallas_call | solution.py:206
  274.6 0.9 copy-done.15
  276.1 49.7 %shard_map.180 = (bf16[1024,384]{1,0:T(8,128)(2,1)}, f32[8,384]{1,0:T(8,128)}, bf16[384,1152]{1,0:T(8,128)(2,1)}, bf16[384,384]{1,0:T(8,128)(2,1)}, bf16[384,153...) custom-call(bf16[1024,384]{1,0:T(8,128)(2,1)} %pad_maximum_fusion.3.g_ref, bf16[1024,384]{1,0:T(8,128)(2,1)} %copy-done.4, ...), custom_call_target="tpu_custom_call" | custom-call | flops 25769803776 | bytes 25165824 | tf_op jit(solution)/shard_map/pallas_call | solution.py:232
  325.9 49.7 %shard_map.181 = (bf16[1024,384]{1,0:T(8,128)(2,1)}, f32[8,384]{1,0:T(8,128)}, bf16[384,1152]{1,0:T(8,128)(2,1)}, bf16[384,384]{1,0:T(8,128)(2,1)}, bf16[384,153...) custom-call(bf16[1024,384]{1,0:T(8,128)(2,1)} %get-tuple-element.43.g_ref, bf16[1024,384]{1,0:T(8,128)(2,1)} %copy-done.3, ...), custom_call_target="tpu_custom_call" | custom-call | flops 25769803776 | bytes 25165824 | tf_op jit(solution)/shard_map/pallas_call | solution.py:232
  378.9 1.3 pad_maximum_fusion
  380.2 3.7 all-to-all-start
  384.1 52.4 %all-gather.6 = f32[32,1,2304]{2,1,0:T(1,128)S(1)} all-gather(f32[1,1,2304]{2,1,0:T(1,128)S(1)} %reshape.68), channel_id=1, replica_groups=mesh['section'=2,'dp'=8,'context'=2] {'dp','section','context'}, dimensions={0}, use_global_device_ids=true | all-gather | bytes 304128 | tf_op jit(solution)/shard_map/all_gather | solution.py:337
  436.4 37.4 %all-gather.7 = f32[32,1,2304]{2,1,0:T(1,128)S(1)} all-gather(f32[1,1,2304]{2,1,0:T(1,128)S(1)} %reshape.70), channel_id=1, replica_groups=mesh['section'=2,'dp'=8,'context'=2] {'dp','section','context'}, dimensions={0}, use_global_device_ids=true | all-gather | bytes 304128 | tf_op jit(solution)/shard_map/all_gather | solution.py:337
  475.2 8.4 %psum.7 = f32[32,48]{1,0:T(8,128)S(1)} all-reduce(f32[32,48]{1,0:T(8,128)S(1)} %fusion), channel_id=1, replica_groups=mesh['section'=2,'dp'=8,'context'=2] {'section'}, use_global_device_ids=true, to_apply=%region_10.11 | all-reduce | flops 1536 | bytes 12288 | tf_op jit(solution)/shard_map/psum | solution.py:343
  483.7 2.4 pad_maximum_fusion.1
  486.1 3.6 all-to-all-start.1
  489.7 1.0 fusion.7
  490.7 2.1 convolution_bitcast_fusion
  493.5 2.0 collective-permute-start.3
  495.5 58.3 %reduce-scatter.27.cloned.1.call-done = bf16[24,1152]{1,0:T(8,128)(2,1)} async-done(((bf16[384,1152]{1,0:T(8,128)(2,1)}), bf16[24,1152]{1,0:T(8,128)(2,1)}) %reduce-scatter.27.cloned.1.call-update) | async-done | bytes 55312
  554.7 1.5 collective-permute-start.2
  557.0 1.9 all_gather.53
  559.7 2.1 all_gather.52
  561.8 53.1 %reduce-scatter.21.cloned.1.call-done = bf16[96,384]{1,0:T(8,128)(2,1)} async-done(((bf16[1536,384]{1,0:T(8,128)(2,1)}), bf16[96,384]{1,0:T(8,128)(2,1)}) %reduce-scatter.21.cloned.1.call-update) | async-done | bytes 73744 | tf_op jit(solution)/shard_map/reduce_scatter | solution.py:321
  614.9 61.2 %reduce-scatter.23.cloned.1.call-done = bf16[96,384]{1,0:T(8,128)(2,1)} async-done(((bf16[1536,384]{1,0:T(8,128)(2,1)}), bf16[96,384]{1,0:T(8,128)(2,1)}) %reduce-scatter.23.cloned.1.call-update) | async-done | bytes 73744 | tf_op jit(solution)/shard_map/reduce_scatter | solution.py:321
  677.0 1.5 collective-permute-start.5
  678.6 58.7 %reduce-scatter.17.cloned.1.call-done = bf16[24,1536]{1,0:T(8,128)(2,1)} async-done(((bf16[384,1536]{1,0:T(8,128)(2,1)}), bf16[24,1536]{1,0:T(8,128)(2,1)}) %reduce-scatter.17.cloned.1.call-update) | async-done | bytes 73744 | tf_op jit(solution)/shard_map/reduce_scatter | solution.py:321
  737.3 61.2 %reduce-scatter.19.cloned.1.call-done = bf16[24,1536]{1,0:T(8,128)(2,1)} async-done(((bf16[384,1536]{1,0:T(8,128)(2,1)}), bf16[24,1536]{1,0:T(8,128)(2,1)}) %reduce-scatter.19.cloned.1.call-update) | async-done | bytes 73744 | tf_op jit(solution)/shard_map/reduce_scatter | solution.py:321
  799.4 1.5 collective-permute-start.4
  800.9 0.9 convert_add_fusion
  801.9 2.0 all_gather.55
  803.9 0.9 convert_add_fusion.1
  804.8 2.0 all_gather.54
  806.8 1.1 copy.51
  808.0 1.1 copy.52
  (122 shorter events, 23.1 us)
Async XLA Ops:
  8.0 19.2 %copy-start = (bf16[1,48,2304]{2,1,0:T(8,128)(2,1)S(1)}, bf16[1,48,2304]{2,1,0:T(8,128)(2,1)}, u32[]{:S(2)}) copy-start(bf16[1,48,2304]{2,1,0:T(8,128)(2,1)} %param.13) | copy-start | bytes 663556
  8.0 23.3 %copy-start.21 = (bf16[1,192,384]{2,1,0:T(8,128)(2,1)S(1)}, bf16[1,192,384]{2,1,0:T(8,128)(2,1)}, u32[]{:S(2)}) copy-start(bf16[1,192,384]{2,1,0:T(8,128)(2,1)} %param.18) | copy-start | bytes 442372
  8.0 90.3 %all-reduce.11.cloned.1.call-start = ((), (), s32[]{:S(2)}) async-start(), calls=%async_computation.17 | async-start | bytes 589824
  27.2 8.3 %copy-start.24 = (bf16[1,48,384]{2,1,0:T(8,128)(2,1)S(1)}, bf16[1,48,384]{2,1,0:T(8,128)(2,1)}, u32[]{:S(2)}) copy-start(bf16[1,48,384]{2,1,0:T(8,128)(2,1)} %param.16) | copy-start | bytes 110596
  28.1 78.3 %all-gather.12.cloned.1.call-start = ((), (), s32[]{:S(2)}) async-start(), calls=%async_computation.14 | async-start | bytes 1824768 | tf_op jit(solution)/shard_map/all_gather | solution.py:293
  29.6 116.8 %all-gather.14.cloned.1.call-start = ((), (), s32[]{:S(2)}) async-start(), calls=%async_computation.15 | async-start | bytes 2433024 | tf_op jit(solution)/shard_map/all_gather | solution.py:293
  31.2 175.0 %all-gather.16.cloned.1.call-start = ((), (), s32[]{:S(2)}) async-start(), calls=%async_computation.16 | async-start | bytes 2433024 | tf_op jit(solution)/shard_map/all_gather | solution.py:293
  32.0 460.8 %reduce-scatter.29.cloned.1.call-start = ((), (), s32[]{:S(2)}) async-start(), calls=%async_computation.20 | async-start | bytes 313344
  33.1 70.9 %collective-permute-start.1 = (bf16[512,384]{1,0:T(8,128)(2,1)S(1)}, bf16[512,384]{1,0:T(8,128)(2,1)S(1)}, u32[]{:S(2)}, u32[]{:S(2)}) collective-permute-start(bf16[512,384]{1,0:T(8,128)(2,1)S(1)} %dynamic-slice_bitcast_fusion), channel_id=1, source_target_pairs={{0,1},{1,0},{2,3},{3,2},{4,5},{5,4},{6,7},{7,6},{8,9},{9,8},{10,11... | collective-permute-start | bytes 1179656 | tf_op jit(solution)/shard_map/ppermute | solution.py:262
  34.2 69.8 %collective-permute-start = (bf16[512,384]{1,0:T(8,128)(2,1)S(1)}, bf16[512,384]{1,0:T(8,128)(2,1)S(1)}, u32[]{:S(2)}, u32[]{:S(2)}) collective-permute-start(bf16[512,384]{1,0:T(8,128)(2,1)S(1)} %dynamic-slice_bitcast_fusion.1), channel_id=1, source_target_pairs={{0,1},{1,0},{2,3},{3,2},{4,5},{5,4},{6,7},{7,6},{8,9},{9,8},{10,11... | collective-permute-start | bytes 1179656 | tf_op jit(solution)/shard_map/ppermute | solution.py:262
  75.9 133.6 %copy-start.6 = (bf16[384,384]{1,0:T(8,128)(2,1)}, bf16[384,384]{1,0:T(8,128)(2,1)S(1)}, u32[]{:S(2)}) copy-start(bf16[384,384]{1,0:T(8,128)(2,1)S(1)} %get-tuple-element.76.wproj) | copy-start | bytes 884740
  75.9 165.9 %copy-start.7 = (bf16[384,384]{1,0:T(8,128)(2,1)}, bf16[384,384]{1,0:T(8,128)(2,1)S(1)}, u32[]{:S(2)}) copy-start(bf16[384,384]{1,0:T(8,128)(2,1)S(1)} %get-tuple-element.75.wproj) | copy-start | bytes 884740
  104.0 105.6 %copy-start.8 = (f32[8,384]{1,0:T(8,128)}, f32[8,384]{1,0:T(8,128)S(1)}, u32[]{:S(2)}) copy-start(f32[8,384]{1,0:T(8,128)S(1)} %get-tuple-element.78.mod_ref) | copy-start | bytes 36868
  104.0 137.9 %copy-start.9 = (f32[8,384]{1,0:T(8,128)}, f32[8,384]{1,0:T(8,128)S(1)}, u32[]{:S(2)}) copy-start(f32[8,384]{1,0:T(8,128)S(1)} %get-tuple-element.77.mod_ref) | copy-start | bytes 36868
  106.3 103.2 %copy-start.3 = (bf16[1024,384]{1,0:T(8,128)(2,1)}, bf16[1024,384]{1,0:T(8,128)(2,1)S(1)}, u32[]{:S(2)}) copy-start(bf16[1024,384]{1,0:T(8,128)(2,1)S(1)} %pad_maximum_fusion.2.x_ref) | copy-start | bytes 2359300
  108.2 101.3 %copy-start.1 = (bf16[384,1152]{1,0:T(8,128)(2,1)}, bf16[384,1152]{1,0:T(8,128)(2,1)S(1)}, u32[]{:S(2)}) copy-start(bf16[384,1152]{1,0:T(8,128)(2,1)S(1)} %get-tuple-element.74.wqkv) | copy-start | bytes 2654212
  108.2 133.6 %copy-start.2 = (bf16[384,1152]{1,0:T(8,128)(2,1)}, bf16[384,1152]{1,0:T(8,128)(2,1)S(1)}, u32[]{:S(2)}) copy-start(bf16[384,1152]{1,0:T(8,128)(2,1)S(1)} %get-tuple-element.73.wqkv) | copy-start | bytes 2654212
  240.1 0.9 copy-start.10
  240.9 0.9 copy-start.11
  241.8 31.0 %copy-start.4 = (bf16[1024,384]{1,0:T(8,128)(2,1)}, bf16[1024,384]{1,0:T(8,128)(2,1)S(1)}, u32[]{:S(2)}) copy-start(bf16[1024,384]{1,0:T(8,128)(2,1)S(1)} %get-tuple-element.35.x_ref) | copy-start | bytes 2359300
  241.8 31.0 %copy-start.12 = (bf16[1024,384]{1,0:T(8,128)(2,1)}, bf16[1024,384]{1,0:T(8,128)(2,1)S(1)}, u32[]{:S(2)}) copy-start(bf16[1024,384]{1,0:T(8,128)(2,1)S(1)} %get-tuple-element.49.mo_ref) | copy-start | bytes 2359300
  241.8 31.0 %copy-start.16 = (f32[8,1024]{1,0:T(8,128)}, f32[8,1024]{1,0:T(8,128)S(1)}, u32[]{:S(2)}) copy-start(f32[8,1024]{1,0:T(8,128)S(1)} %get-tuple-element.45.lse_ref) | copy-start | bytes 98308
  272.8 0.9 copy-start.13
  273.7 0.9 copy-start.14
  274.6 0.9 copy-start.15
  275.5 0.6 copy-start.17
  325.9 166.9 %reduce-scatter.31.cloned.1.call-start = ((), (), s32[]{:S(2)}) async-start(), calls=%async_computation.21 | async-start | bytes 313344
  375.7 119.8 %reduce-scatter.25.cloned.1.call-start = ((), (), s32[]{:S(2)}) async-start(), calls=%async_computation.18 | async-start | bytes 940032
  376.3 177.6 %reduce-scatter.27.cloned.1.call-start = ((), (), s32[]{:S(2)}) async-start(), calls=%async_computation.19 | async-start | bytes 940032
  376.9 238.0 %reduce-scatter.21.cloned.1.call-start = ((), (), s32[]{:S(2)}) async-start(), calls=%async_computation.12 | async-start | bytes 1253376 | tf_op jit(solution)/shard_map/reduce_scatter | solution.py:321
  376.9 2.0 copy-start.5
  377.4 298.7 %reduce-scatter.23.cloned.1.call-start = ((), (), s32[]{:S(2)}) async-start(), calls=%async_computation.13 | async-start | bytes 1253376 | tf_op jit(solution)/shard_map/reduce_scatter | solution.py:321
  378.2 359.1 %reduce-scatter.17.cloned.1.call-start = ((), (), s32[]{:S(2)}) async-start(), calls=%async_computation.10 | async-start | bytes 1253376 | tf_op jit(solution)/shard_map/reduce_scatter | solution.py:321
  380.2 3.8 copy-start.23
  380.2 3.8 copy-start.22
  380.2 105.9 %all-to-all-start = ((bf16[4,512,384]{2,1,0:T(8,128)(2,1)}), bf16[4,512,384]{2,1,0:T(8,128)(2,1)S(1)}, u32[]{:S(2)}, u32[]{:S(2)}) async-start(bf16[4,512,384]{2,1,0:T(8,128)(2,1)} %bitcast.61), calls=%async_computation | async-start | bytes 3145728 | tf_op jit(solution)/shard_map/all_to_all | solution.py:276
  383.9 414.6 %reduce-scatter.19.cloned.1.call-start = ((), (), s32[]{:S(2)}) async-start(), calls=%async_computation.11 | async-start | bytes 1253376 | tf_op jit(solution)/shard_map/reduce_scatter | solution.py:321
  384.1 99.6 %copy-start.20 = (bf16[1024,384]{1,0:T(8,128)(2,1)S(1)}, bf16[1024,384]{1,0:T(8,128)(2,1)}, u32[]{:S(2)}) copy-start(bf16[1024,384]{1,0:T(8,128)(2,1)} %get-tuple-element.43.g_ref) | copy-start | bytes 2359300
  474.2 11.9 %copy-start.18 = (f32[32,1,2304]{2,1,0:T(1,128)}, f32[32,1,2304]{2,1,0:T(1,128)S(1)}, u32[]{:S(2)}) copy-start(f32[32,1,2304]{2,1,0:T(1,128)S(1)} %get-tuple-element.64) | copy-start | bytes 884740
  486.1 72.7 %all-to-all-start.1 = ((bf16[4,512,384]{2,1,0:T(8,128)(2,1)}), bf16[4,512,384]{2,1,0:T(8,128)(2,1)S(1)}, u32[]{:S(2)}, u32[]{:S(2)}) async-start(bf16[4,512,384]{2,1,0:T(8,128)(2,1)} %bitcast.60), calls=%async_computation.1 | async-start | bytes 3145728 | tf_op jit(solution)/shard_map/all_to_all | solution.py:276
  493.5 62.7 %collective-permute-start.3 = (bf16[24,384]{1,0:T(8,128)(2,1)S(1)}, bf16[24,384]{1,0:T(8,128)(2,1)S(1)}, u32[]{:S(2)}, u32[]{:S(2)}) collective-permute-start(bf16[24,384]{1,0:T(8,128)(2,1)S(1)} %broadcast_select_fusion.4), channel_id=1, source_target_pairs={{0,16},{16,0},{1,17},{17,1},{2,18},{18,2},{3,19},{19,3},{4,20},{20... | collective-permute-start | bytes 55304 | tf_op jit(solution)/shard_map/ppermute | solution.py:262
  554.7 4.2 collective-permute-start.2
  677.0 123.9 %collective-permute-start.5 = (bf16[96,384]{1,0:T(8,128)(2,1)S(1)}, bf16[96,384]{1,0:T(8,128)(2,1)}, u32[]{:S(2)}, u32[]{:S(2)}) collective-permute-start(bf16[96,384]{1,0:T(8,128)(2,1)S(1)} %broadcast_select_fusion.1), channel_id=1, source_target_pairs={{0,16},{16,0},{1,17},{17,1},{2,18},{18,2},{3,19},{19,3},{4,20},{20... | collective-permute-start | bytes 221192 | tf_op jit(solution)/shard_map/ppermute | solution.py:262
  799.4 4.5 collective-permute-start.4
  808.0 1.1 copy-start.19
Sparse Core Ops, SparseCore 0:
  28.2 70.0 all-reduce.10
  326.0 52.7 reduce-scatter.28
  382.9 52.8 reduce-scatter.30
  439.6 55.0 reduce-scatter.24
  498.7 55.1 reduce-scatter.26
  557.7 57.0 reduce-scatter.20
  618.9 57.1 reduce-scatter.22
  680.2 57.0 reduce-scatter.16
  741.4 57.0 reduce-scatter.18
Sparse Core Ops, SparseCore 1:
  32.4 54.1 all-gather.11
  90.3 56.1 all-gather.13
  150.2 56.0 all-gather.15

commit v2 on v1

--- a/solution.py
+++ b/solution.py
@@ -104,8 +104,8 @@
 
 
 def bwd_kernel(g_ref, x_ref, mod_ref, wqkv, wproj, wmi, wmo, qkv_ref, lse_ref, mix_ref, mid_ref, ao_ref, mo_ref,
-               gin_ref, gmod_ref, dqkvw_ref, dproj_ref, dmi_ref, dmo_ref,
-               aqkv, aproj, ami, amo, kt_ref, gmid_ref, gmx_ref, delta_ref, dqkv_ref, dk_acc, dv_acc):
+               gin_ref, gmod_ref, aqkv, aproj, ami, amo,
+               kt_ref, gmid_ref, gmx_ref, delta_ref, dqkv_ref, dk_acc, dv_acc):
     tok, d = x_ref.shape
     heads = d // HDIM
     mod = mod_ref[...]
@@ -189,10 +189,6 @@
         gin_ref[rows, :] = (gmid_ref[rows, :] + norm_back(n, rs, gf * (1.0 + sc1))).astype(BF16)
 
     row_loop(tok, project_back)
-    dqkvw_ref[...] = aqkv[...].astype(BF16)
-    dproj_ref[...] = aproj[...].astype(BF16)
-    dmi_ref[...] = ami[...].astype(BF16)
-    dmo_ref[...] = amo[...].astype(BF16)
 
 
 def vmem(count):
@@ -231,11 +227,10 @@
     shapes = [(d, 3 * d), (d, d), (d, ff), (ff, d)]
     return pl.pallas_call(
         bwd_kernel,
-        out_shape=[sds((tok, d), BF16), sds((8, d), F32)] + [sds(s, BF16) for s in shapes],
+        out_shape=[sds((tok, d), BF16), sds((8, d), F32)] + [sds(s, F32) for s in shapes],
         in_specs=vmem(13),
         out_specs=vmem(6),
-        scratch_shapes=[pltpu.VMEM(s, F32) for s in shapes]
-        + [
+        scratch_shapes=[
             pltpu.VMEM((d, tok), BF16),
             pltpu.VMEM((tok, d), F32),
             pltpu.VMEM((tok, d), BF16),
@@ -286,16 +281,20 @@
     steps_all = lax.all_gather(timesteps, "dp", tiled=True)
     labels_all = lax.all_gather(labels, "dp", tiled=True)
 
-    def gather(w):
-        w = w[0]
-        half = w.shape[0] // 2
-        mine = lax.dynamic_slice_in_dim(w, context * half, half, 0)
-        full = lax.all_gather(mine, ("section", "dp", "context"), axis=0, tiled=True)
-        rows = full.shape[0] // 2
-        return full[:rows], full[rows:]
-
-    pairs = [gather(w) for w in (qkv_w, proj_w, mlp_in_w, mlp_out_w)]
-    weights = [tuple(pair[layer] for pair in pairs) for layer in range(2)]
+    half = qkv_w.shape[1] // 2
+    packed = jnp.concatenate(
+        [w[0].reshape(2 * half, -1) for w in (qkv_w, proj_w, mlp_in_w, mlp_out_w)], axis=1
+    )
+    packed = lax.dynamic_slice_in_dim(packed, context * half, half, 0)
+    packed = lax.all_gather(packed, ("section", "dp", "context"), axis=0, tiled=True)
+    packed = packed.reshape(2, d, packed.shape[1])
+    ff = mlp_in_w.shape[2]
+
+    def unpack(block):
+        parts = jnp.split(block, [3 * d, 4 * d, 4 * d + ff], axis=1)
+        return parts[:3] + [parts[3].reshape(-1, d)]
+
+    weights = [unpack(packed[layer]) for layer in range(2)]
     hidden = take_latent(hidden_in, section, context)
     cot = take_latent(cotangent, section, context)
 
@@ -318,25 +317,23 @@
     states = spread_out(passed, second)
 
     def reduce(grads):
-        return [lax.psum_scatter(g, ("dp", "context"), scatter_dimension=0, tiled=True) for g in grads]
+        flat = jnp.concatenate([g.reshape(d, -1) for g in grads], axis=1)
+        return lax.psum_scatter(flat, ("dp", "context"), scatter_dimension=0, tiled=True)
 
     g0, gmod1, *wg1 = run_backward(cot, passed, mods[1], weights[1], saved1)
-    parts1 = reduce(wg1)
+    part1 = reduce(wg1)
     gin, gmod0, *wg0 = run_backward(g0, hidden, mods[0], weights[0], saved0)
-    parts0 = reduce(wg0)
+    part0 = reduce(wg0)
     grads = spread_out(gin, g0)
 
     upper = section == 1
-    shares = []
-    for p0, p1 in zip(parts0, parts1):
-        other = swap_axis(jnp.where(upper, p0, p1), "section")
-        mine = jnp.where(upper, p1, p0).astype(F32) + other.astype(F32)
-        shares.append(lax.all_gather(mine, "context", axis=0, tiled=True)[None])
-
-    def all_latents(gmod):
-        return lax.all_gather(gmod[:6].reshape(-1), ("dp", "section", "context"))
-
-    gm = jnp.where(upper, all_latents(gmod1), all_latents(gmod0))
+    other = swap_axis(jnp.where(upper, part0, part1).astype(BF16), "section")
+    mine = jnp.where(upper, part1, part0) + other.astype(F32)
+    shares = [share[None] for share in unpack(lax.all_gather(mine, "context", axis=0, tiled=True))]
+
+    gmods = jnp.stack([gmod0[:6].reshape(-1), gmod1[:6].reshape(-1)])
+    gmods = lax.all_gather(gmods, ("dp", "section", "context"))
+    gm = lax.dynamic_index_in_dim(gmods, section, 1, keepdims=False)
     grad_ada = jnp.einsum("ld,le->de", silu_low.astype(F32), gm, precision=HIGH)[None]
     grad_bias = lax.dynamic_slice_in_dim(jnp.sum(gm, axis=0, keepdims=True), dp * wide, wide, 1)
     grad_silu = jnp.einsum("le,de->ld", gm, ada_w[0].astype(F32), precision=HIGH)

time: 824 us -> 468 us (0.57)
  waiting for transfers between devices: 413 us -> 130 us
  blocking collectives: 164 us -> 81 us
    reduce_scatter x4 -> x2, waiting for transfers between devices: 234 us -> 49.4 us  [reduce(): lax.psum_scatter(flat, ('dp', 'context'), scatter_dimension=0, tiled=True)]
    all_gather x3 -> x1, waiting for transfers between devices: 94.8 us -> 0.01 us  [per_device(): lax.all_gather(packed, ('section', 'dp', 'context'), axis=0, tiled=True)]
    all_gather x7 -> x2, blocking collectives: 138 us -> 56.6 us  [the longest x1 54.1 us: per_device(): gmods = lax.all_gather(gmods, ('dp', 'section', 'context'))]
    concatenate x0 -> x3, other arithmetic: none -> 11.3 us  [the longest x2 9.63 us: reduce(): flat = jnp.concatenate([g.reshape(d, -1) for g in grads], axis=1)]
    reshape x0 -> x4, local copies, waits for them, and re-layouts: none -> 9.67 us  [the longest x2 4.87 us: reduce(): flat = jnp.concatenate([g.reshape(d, -1) for g in grads], axis=1)]
    slice x4 -> x0, local copies, waits for them, and re-layouts: 8.38 us -> none  [gather(): return (full[:rows], full[rows:])]
    split x0 -> x4, local copies, waits for them, and re-layouts: none -> 8.25 us  [unpack(): parts = jnp.split(block, [3 * d, 4 * d, 4 * d + ff], axis=1)]
    unnamed x17 -> x5, waiting for transfers between devices: 83.8 us -> 75.9 us
  transfers between devices with their start and end apart: 20 -> 9, of which waited for: 9 -> 3; matrix products, arithmetic and copies ran while one was open for 3% -> 5% of each run, Pallas kernels for 6% -> 11%
where the time goes in v2:
time: 468 us; the launch traced here: 464 us
  Pallas kernels  163 us (35%)
  waiting for transfers between devices  130 us (28%)
  blocking collectives  81 us (17%)
  local copies, waits for them, and re-layouts  37.1 us (8%)
  other arithmetic  20.5 us (4%)
  between operations  17.4 us (4%)
  starting transfers between devices  9.36 us (2%)
  matrix products  5.41 us (1%)
    pallas_call x2, Pallas kernels, run_backward(): pl.pallas_call(bwd_kernel, out_shape=[sds((tok, d), BF16), sds((8, d), F3...  102 us
    unnamed x5, waiting for transfers between devices  75.9 us
    pallas_call x2, Pallas kernels, run_forward(): pl.pallas_call(fwd_kernel, out_shape=[sds((tok, d), BF16), sds((tok, 3 *...  61.5 us
    all_gather x1, blocking collectives, per_device(): gmods = lax.all_gather(gmods, ('dp', 'section', 'context'))  54.1 us
    reduce_scatter x2, waiting for transfers between devices, reduce(): lax.psum_scatter(flat, ('dp', 'context'), scatter_dimension=0, tiled=True)  49.4 us
    unnamed x1, blocking collectives  13.1 us
    unnamed x60, local copies, waits for them, and re-layouts  12.9 us
    concatenate x2, other arithmetic, reduce(): flat = jnp.concatenate([g.reshape(d, -1) for g in grads], axis=1)  9.63 us
  transfers between devices with their start and end apart: 9, of which 3 were waited for; matrix products, arithmetic and copies ran while one was open for 5% of the time, Pallas kernels for 11%

profile of v2, /device:TPU:0, one launch (start us, length us, event | category | flops | bytes accessed | tf_op | source)
XLA Modules:
  0.0 463.9 jit_solution(5527421378034239505)
XLA Ops:
  8.1 1.4 fusion.28
  10.2 0.9 dynamic-update-slice
  11.9 13.1 %all-reduce.4 = (s32[32]{0:T(128)S(1)}, s32[32]{0:T(128)S(1)}) all-reduce(s32[32]{0:T(128)S(1)} %dynamic-update-slice.1, s32[32]{0:T(128)S(1)} %dynamic-update-slice), channel_id=1, replica_groups=mesh['section'=2,'dp'=8,'context'=2] {'dp'}, use_global_device_ids=true, to_apply=%add.2 | all-reduce | flops 64 | bytes 512
  26.1 1.1 convolution_add_fusion.1
  27.2 0.9 convolution_add_fusion
  28.2 1.0 reshape_squeeze.3
  29.2 1.6 fusion.7
  31.0 1.1 dynamic-slice_bitcast_fusion.1
  33.4 75.8 %all-reduce.7.cloned.1.call-done = f32[32,2304]{1,0:T(8,128)} async-done(((f32[32,2304]{1,0:T(8,128)}), f32[32,2304]{1,0:T(8,128)}) %all-reduce.7.cloned.1.call-update) | async-done | bytes 294928
  109.2 0.9 dynamic-slice_bitcast_fusion.2
  110.1 4.6 all-gather.2
  114.8 1.3 bitcast_select_fusion.1
  116.2 1.1 pad_maximum_fusion.5.g_ref
  117.3 4.2 fusion.24
  121.6 3.3 reshape.57.wmo
  124.8 1.5 reshape.58.wmo
  126.4 1.6 fusion.26
  128.0 1.6 fusion.25
  129.6 30.6 %shard_map.178 = (bf16[1024,384]{1,0:T(8,128)(2,1)S(1)}, bf16[1024,1152]{1,0:T(8,128)(2,1)}, f32[8,1024]{1,0:T(8,128)S(1)}, bf16[1024,384]{1,0:T(8,128)(2,1)S(1)...) custom-call(bf16[1024,384]{1,0:T(8,128)(2,1)S(1)} %pad_maximum_fusion.4.x_ref, ...), custom_call_target="tpu_custom_call" | custom-call | flops 10066329600 | bytes 16777216 | tf_op jit(solution)/shard_map/pallas_call | solution.py:202
  160.2 0.9 copy-done.10
  161.1 0.9 copy-done.11
  162.1 30.9 %shard_map.179 = (bf16[1024,384]{1,0:T(8,128)(2,1)S(1)}, bf16[1024,1152]{1,0:T(8,128)(2,1)}, f32[8,1024]{1,0:T(8,128)S(1)}, bf16[1024,384]{1,0:T(8,128)(2,1)S(1)...) custom-call(bf16[1024,384]{1,0:T(8,128)(2,1)S(1)} %get-tuple-element.35.x_ref, ...), custom_call_target="tpu_custom_call" | custom-call | flops 10066329600 | bytes 16777216 | tf_op jit(solution)/shard_map/pallas_call | solution.py:202
  193.1 0.9 copy-done.13
  194.0 0.9 copy-done.14
  194.9 0.9 copy-done.15
  196.4 50.7 %shard_map.180 = (bf16[1024,384]{1,0:T(8,128)(2,1)}, f32[8,384]{1,0:T(8,128)}, f32[384,1152]{1,0:T(8,128)}, f32[384,384]{1,0:T(8,128)}, f32[384,1536]{1,0:T(8,128)}, /*index=5*/f32[1536,384]{1,0:T(8,128)}) custom-call(bf16[1024,384]{1,0:T(8,128)(2,1)} %pad_maximum_fusion.5.g_ref, bf16[1024,384]{1,0:T(8,128)(2,1)} %copy-done.4, f32[8,384]{1,0:T(8,128)} %copy-done.9, ...), custom_call_target="tpu_custom_call" | custom-call | flops 25769803776 | bytes 25165824 | tf_op jit(solution)/shard_map/pallas_call | solution.py:228
  247.1 2.4 reshape.61
  249.5 4.8 %pad_maximum_fusion = f32[384,4608]{1,0:T(8,128)} fusion(f32[384,1536]{1,0:T(8,128)S(1)} %reshape.61, f32[384,1536]{1,0:T(8,128)} %get-tuple-element.55, f32[384,384]{1,0:T(8,128)} %get-tuple-element.54, f32[384,1152]{1,0:T(8,128)} %get-tuple-element.53), kind=kLoop, calls=%fused_computation | loop fusion | flops 5308416 | bytes 14155776 | tf_op jit(solution)/shard_map/concatenate | solution.py:320
  254.4 50.9 %shard_map.181 = (bf16[1024,384]{1,0:T(8,128)(2,1)}, f32[8,384]{1,0:T(8,128)}, f32[384,1152]{1,0:T(8,128)}, f32[384,384]{1,0:T(8,128)}, f32[384,1536]{1,0:T(8,128)}, /*index=5*/f32[1536,384]{1,0:T(8,128)}) custom-call(bf16[1024,384]{1,0:T(8,128)(2,1)} %get-tuple-element.43.g_ref, bf16[1024,384]{1,0:T(8,128)(2,1)} %copy-done.3, f32[8,384]{1,0:T(8,128)} %copy-done.8, ...), custom_call_target="tpu_custom_call" | custom-call | flops 25769803776 | bytes 25165824 | tf_op jit(solution)/shard_map/pallas_call | solution.py:228
  305.3 2.4 reshape.62
  307.8 4.8 %pad_maximum_fusion.1 = f32[384,4608]{1,0:T(8,128)} fusion(f32[384,1536]{1,0:T(8,128)S(1)} %reshape.62, f32[384,1536]{1,0:T(8,128)} %get-tuple-element.59, f32[384,384]{1,0:T(8,128)} %get-tuple-element.58, f32[384,1152]{1,0:T(8,128)} %get-tuple-element.57), kind=kLoop, calls=%fused_computation.1 | loop fusion | flops 5308416 | bytes 14155776 | tf_op jit(solution)/shard_map/concatenate | solution.py:320
  314.0 1.3 pad_maximum_fusion.3
  315.3 3.6 all-to-all-start.1
  318.9 54.1 %all-gather.3 = f32[32,2,2304]{2,1,0:T(2,128)S(1)} all-gather(f32[1,2,2304]{2,1,0:T(2,128)S(1)} %maximum_bitcast_fusion), channel_id=3, replica_groups=mesh['section'=2,'dp'=8,'context'=2] {'dp','section','context'}, dimensions={0}, use_global_device_ids=true | all-gather | bytes 608256 | tf_op jit(solution)/shard_map/all_gather | solution.py:335
  374.4 6.7 %psum.7 = f32[32,48]{1,0:T(8,128)S(1)} all-reduce(f32[32,48]{1,0:T(8,128)S(1)} %fusion), channel_id=1, replica_groups=mesh['section'=2,'dp'=8,'context'=2] {'section'}, use_global_device_ids=true, to_apply=%region_4.5 | all-reduce | flops 1536 | bytes 12288 | tf_op jit(solution)/shard_map/psum | solution.py:340
  381.1 2.1 convolution_bitcast_fusion
  383.3 1.3 pad_maximum_fusion.2
  384.6 3.6 all-to-all-start
  388.2 49.3 %reduce-scatter.5.cloned.1.call-done = f32[24,4608]{1,0:T(8,128)} async-done(((f32[384,4608]{1,0:T(8,128)}), f32[24,4608]{1,0:T(8,128)}) %reduce-scatter.5.cloned.1.call-update) | async-done | bytes 442384 | tf_op jit(solution)/shard_map/reduce_scatter | solution.py:321
  437.5 1.7 select_convert_fusion
  439.2 1.4 collective-permute-start.2
  440.7 1.0 fusion.10
  441.7 4.8 %collective-permute-done.2 = bf16[24,4608]{1,0:T(8,128)(2,1)} collective-permute-done((bf16[24,4608]{1,0:T(8,128)(2,1)}, bf16[24,4608]{1,0:T(8,128)(2,1)}, u32[]{:S(2)}, u32[]{:S(2)}) %collective-permute-start.2) | collective-permute-done | bytes 221216 | tf_op jit(solution)/shard_map/ppermute | solution.py:257
  446.5 1.2 convert_add_fusion
  447.6 2.4 all_gather.31
  452.3 1.8 broadcast_in_dim_reshape.3
  454.0 1.1 copy.49
  455.2 1.1 copy.50
  (85 shorter events, 8.7 us)
Async XLA Ops:
  8.0 19.2 %copy-start = (bf16[1,48,2304]{2,1,0:T(8,128)(2,1)S(1)}, bf16[1,48,2304]{2,1,0:T(8,128)(2,1)}, u32[]{:S(2)}) copy-start(bf16[1,48,2304]{2,1,0:T(8,128)(2,1)} %param.13) | copy-start | bytes 663556
  8.0 24.1 %copy-start.21 = (bf16[4,512,384]{2,1,0:T(8,128)(2,1)S(1)}, bf16[4,512,384]{2,1,0:T(8,128)(2,1)}, u32[]{:S(2)}) copy-start(bf16[4,512,384]{2,1,0:T(8,128)(2,1)} %param.12) | copy-start | bytes 4718596
  8.0 101.1 %all-reduce.7.cloned.1.call-start = ((), (), s32[]{:S(2)}) async-start(), calls=%async_computation.7 | async-start | bytes 589824
  28.2 89.2 %all-gather.6.cloned.1.call-start = ((), (), s32[]{:S(2)}) async-start(), calls=%async_computation.4 | async-start | bytes 7299072 | tf_op jit(solution)/shard_map/all_gather | solution.py:289
  30.9 357.3 %reduce-scatter.3.cloned.1.call-start = ((), (), s32[]{:S(2)}) async-start(), calls=%async_computation.5 | async-start | bytes 7520256 | tf_op jit(solution)/shard_map/reduce_scatter | solution.py:321
  32.0 82.8 %collective-permute-start = (bf16[512,384]{1,0:T(8,128)(2,1)S(1)}, bf16[512,384]{1,0:T(8,128)(2,1)S(1)}, u32[]{:S(2)}, u32[]{:S(2)}) collective-permute-start(bf16[512,384]{1,0:T(8,128)(2,1)S(1)} %dynamic-slice_bitcast_fusion.1), channel_id=1, source_target_pairs={{0,1},{1,0},{2,3},{3,2},{4,5},{5,4},{6,7},{7,6},{8,9},{9,8},{10,11... | collective-permute-start | bytes 1179656 | tf_op jit(solution)/shard_map/ppermute | solution.py:257
  32.2 82.7 %collective-permute-start.1 = (bf16[512,384]{1,0:T(8,128)(2,1)S(1)}, bf16[512,384]{1,0:T(8,128)(2,1)}, u32[]{:S(2)}, u32[]{:S(2)}) collective-permute-start(bf16[512,384]{1,0:T(8,128)(2,1)S(1)} %dynamic-slice_bitcast_fusion), channel_id=1, source_target_pairs={{0,1},{1,0},{2,3},{3,2},{4,5},{5,4},{6,7},{7,6},{8,9},{9,8},{10,11... | collective-permute-start | bytes 1179656 | tf_op jit(solution)/shard_map/ppermute | solution.py:257
  114.8 14.8 %copy-start.8 = (f32[8,384]{1,0:T(8,128)}, f32[8,384]{1,0:T(8,128)S(1)}, u32[]{:S(2)}) copy-start(f32[8,384]{1,0:T(8,128)S(1)} %get-tuple-element.80.mod_ref) | copy-start | bytes 36868
  114.8 47.2 %copy-start.9 = (f32[8,384]{1,0:T(8,128)}, f32[8,384]{1,0:T(8,128)S(1)}, u32[]{:S(2)}) copy-start(f32[8,384]{1,0:T(8,128)S(1)} %get-tuple-element.79.mod_ref) | copy-start | bytes 36868
  116.2 13.4 %copy-start.3 = (bf16[1024,384]{1,0:T(8,128)(2,1)}, bf16[1024,384]{1,0:T(8,128)(2,1)S(1)}, u32[]{:S(2)}) copy-start(bf16[1024,384]{1,0:T(8,128)(2,1)S(1)} %pad_maximum_fusion.4.x_ref) | copy-start | bytes 2359300
  127.9 32.2 %copy-start.1 = (bf16[384,1152]{1,0:T(8,128)(2,1)}, bf16[384,1152]{1,0:T(8,128)(2,1)S(1)}, u32[]{:S(2)}) copy-start(bf16[384,1152]{1,0:T(8,128)(2,1)S(1)} %get-tuple-element.72.wqkv) | copy-start | bytes 2654212
  127.9 34.1 %copy-start.2 = (bf16[384,1152]{1,0:T(8,128)(2,1)}, bf16[384,1152]{1,0:T(8,128)(2,1)S(1)}, u32[]{:S(2)}) copy-start(bf16[384,1152]{1,0:T(8,128)(2,1)S(1)} %get-tuple-element.71.wqkv) | copy-start | bytes 2654212
  129.5 30.6 %copy-start.6 = (bf16[384,384]{1,0:T(8,128)(2,1)}, bf16[384,384]{1,0:T(8,128)(2,1)S(1)}, u32[]{:S(2)}) copy-start(bf16[384,384]{1,0:T(8,128)(2,1)S(1)} %get-tuple-element.70.wproj) | copy-start | bytes 884740
  129.6 32.5 %copy-start.7 = (bf16[384,384]{1,0:T(8,128)(2,1)}, bf16[384,384]{1,0:T(8,128)(2,1)S(1)}, u32[]{:S(2)}) copy-start(bf16[384,384]{1,0:T(8,128)(2,1)S(1)} %get-tuple-element.69.wproj) | copy-start | bytes 884740
  160.2 0.9 copy-start.10
  161.1 0.9 copy-start.11
  162.1 31.0 %copy-start.4 = (bf16[1024,384]{1,0:T(8,128)(2,1)}, bf16[1024,384]{1,0:T(8,128)(2,1)S(1)}, u32[]{:S(2)}) copy-start(bf16[1024,384]{1,0:T(8,128)(2,1)S(1)} %get-tuple-element.35.x_ref) | copy-start | bytes 2359300
  162.1 31.0 %copy-start.12 = (bf16[1024,384]{1,0:T(8,128)(2,1)}, bf16[1024,384]{1,0:T(8,128)(2,1)S(1)}, u32[]{:S(2)}) copy-start(bf16[1024,384]{1,0:T(8,128)(2,1)S(1)} %get-tuple-element.49.mo_ref) | copy-start | bytes 2359300
  162.1 31.0 %copy-start.16 = (f32[8,1024]{1,0:T(8,128)}, f32[8,1024]{1,0:T(8,128)S(1)}, u32[]{:S(2)}) copy-start(f32[8,1024]{1,0:T(8,128)S(1)} %get-tuple-element.45.lse_ref) | copy-start | bytes 98308
  193.0 1.0 copy-start.13
  194.0 0.9 copy-start.14
  194.9 0.9 copy-start.15
  195.8 0.6 copy-start.17
  254.3 183.2 %reduce-scatter.5.cloned.1.call-start = ((), (), s32[]{:S(2)}) async-start(), calls=%async_computation.6 | async-start | bytes 7520256 | tf_op jit(solution)/shard_map/reduce_scatter | solution.py:321
  312.6 0.7 copy-start.23
  312.6 0.7 copy-start.22
  312.6 1.2 copy-start.19
  312.6 1.4 copy-start.20
  315.3 69.3 %all-to-all-start.1 = ((bf16[4,512,384]{2,1,0:T(8,128)(2,1)}), bf16[4,512,384]{2,1,0:T(8,128)(2,1)S(1)}, u32[]{:S(2)}, u32[]{:S(2)}) async-start(bf16[4,512,384]{2,1,0:T(8,128)(2,1)} %bitcast.56), calls=%async_computation.1 | async-start | bytes 3145728 | tf_op jit(solution)/shard_map/all_to_all | solution.py:271
  318.9 64.4 %copy-start.5 = (bf16[1024,384]{1,0:T(8,128)(2,1)S(1)}, bf16[1024,384]{1,0:T(8,128)(2,1)}, u32[]{:S(2)}) copy-start(bf16[1024,384]{1,0:T(8,128)(2,1)} %copy-done.4) | copy-start | bytes 2359300
  373.4 0.7 copy-start.18
  384.6 57.1 %all-to-all-start = ((bf16[4,512,384]{2,1,0:T(8,128)(2,1)}), bf16[4,512,384]{2,1,0:T(8,128)(2,1)S(1)}, u32[]{:S(2)}, u32[]{:S(2)}) async-start(bf16[4,512,384]{2,1,0:T(8,128)(2,1)} %bitcast.57), calls=%async_computation | async-start | bytes 3145728 | tf_op jit(solution)/shard_map/all_to_all | solution.py:271
  439.2 7.2 %collective-permute-start.2 = (bf16[24,4608]{1,0:T(8,128)(2,1)}, bf16[24,4608]{1,0:T(8,128)(2,1)}, u32[]{:S(2)}, u32[]{:S(2)}) collective-permute-start(bf16[24,4608]{1,0:T(8,128)(2,1)} %select_convert_fusion), channel_id=1, source_target_pairs={{0,16},{16,0},{1,17},{17,1},{2,18},{18,2},{3,19},{19,3},{4,20},{20... | collective-permute-start | bytes 663560 | tf_op jit(solution)/shard_map/ppermute | solution.py:257
Sparse Core Ops, SparseCore 0:
  28.3 80.8 all-reduce.6
  254.5 88.8 reduce-scatter.2
  347.4 90.0 reduce-scatter.4
Sparse Core Ops, SparseCore 1:
  32.5 71.1 all-gather.5
